TPU v7x, 512 devices: a whole 4x4x16 slice. The times are simulated.
512 devices in a mesh: section: 16 (over z_hi, y, core), tp: 32 (over x, z_lo).
Axes of the slice: x: 4, y: 4, z: 16 (z_hi: 2, z_lo: 8; z = z_hi * 8 + z_lo), core: 2. Of those that a mesh axis runs over, the one named last changes fastest.
Arguments:
- qkv_sent: bfloat16 [16, 768, 3, 12288], P('section', None, None, 'tp'), may hold values from -5 to 5, as said below
- grad_out: bfloat16 [16, 768, 12288], P('section', None, 'tp'), may hold values from -6 to 6
Outputs:
- attn_out: bfloat16 [16, 768, 12288], P('section', None, 'tp')
- grad_qkv: bfloat16 [16, 768, 3, 12288], P('section', None, None, 'tp')
Inputs may be any that keep to these rules, and one draw needn't show every extreme that they name: `qkv_sent`: entries of the queries, keys and values are real values.
All inputs are finite; a program needn't handle non-finite values.
Results may differ from a plain program's by a relative error of at most 0.014.
Values may be sent and summed in bfloat16 or wider, within the bound.
No kernel may reach another device: no remote copies, remote signals or barrier semaphores. Data moves between devices by JAX's collectives and lax.ppermute only.
A program may use at most 64 MiB of HBM per device.

v0:
```python
import math

import jax
import jax.numpy as jnp
from jax import lax
from jax.sharding import PartitionSpec as P

HD = 128


def from_behind(value, axis, steps):
    count = lax.axis_size(axis)
    pairs = [(source, (source + steps) % count) for source in range(count)]
    return lax.ppermute(value, axis, pairs)


def on_device(qkv_sent, grad_out):
    length = qkv_sent.shape[1]
    heads_local = qkv_sent.shape[3] // HD
    local = qkv_sent[0].reshape(length, 3, heads_local, HD)
    dout = grad_out[0].reshape(length, heads_local, HD)
    arrived = from_behind(local, "section", 1)
    query = arrived[:, 0]
    keys = arrived[:, 1]
    values = arrived[:, 2]
    scale = 1.0 / math.sqrt(HD)
    rows = lax.broadcasted_iota(jnp.int32, (length, length), 0)
    cols = lax.broadcasted_iota(jnp.int32, (length, length), 1)
    causal = (cols <= rows)[None]
    scores = jnp.einsum("qhd,khd->hqk", query, keys, preferred_element_type=jnp.float32) * scale
    scores = jnp.where(causal, scores, -jnp.inf)
    peak = jnp.max(scores, axis=2, keepdims=True)
    expo = jnp.exp(scores - peak)
    probs = expo / jnp.sum(expo, axis=2, keepdims=True)
    weights = probs.astype(jnp.bfloat16)
    output = jnp.einsum("hqk,khd->qhd", weights, values, preferred_element_type=jnp.float32).astype(
        jnp.bfloat16
    )
    grad_v = jnp.einsum("hqk,qhd->khd", weights, dout, preferred_element_type=jnp.float32).astype(
        jnp.bfloat16
    )
    grad_p = jnp.einsum("qhd,khd->hqk", dout, values, preferred_element_type=jnp.float32)
    delta = jnp.sum(dout.astype(jnp.float32) * output.astype(jnp.float32), axis=2)
    grad_s = (probs * (grad_p - delta.T[:, :, None])).astype(jnp.bfloat16)
    grad_q = (
        jnp.einsum("hqk,khd->qhd", grad_s, keys, preferred_element_type=jnp.float32) * scale
    ).astype(jnp.bfloat16)
    grad_k = (
        jnp.einsum("hqk,qhd->khd", grad_s, query, preferred_element_type=jnp.float32) * scale
    ).astype(jnp.bfloat16)
    grads = jnp.stack([grad_q, grad_k, grad_v], axis=1)
    returned = from_behind(grads, "section", -1)
    attn_out = output.reshape(1, length, heads_local * HD)
    grad_qkv = returned.reshape(1, length, 3, heads_local * HD)
    return (attn_out, grad_qkv)


def solution(mesh):
    in_specs = (P("section", None, None, "tp"), P("section", None, "tp"))
    out_specs = (P("section", None, "tp"), P("section", None, None, "tp"))
    return jax.shard_map(
        on_device, mesh=mesh, in_specs=in_specs, out_specs=out_specs, check_vma=False
    )
```

profile of v0, /device:TPU:89, one launch (start us, length us, event | category | flops | bytes accessed | tf_op | source)
XLA Modules:
  0.0 208.1 jit_solution(6265446203846413830)
XLA Ops:
  0.6 2.6 %copy.12 = bf16[1,768,3,384]{1,3,2,0:T(8,128)(2,1)S(1)} copy(bf16[1,768,3,384]{3,1,2,0:T(8,128)(2,1)} %param.2) | data formatting | bytes 3538944 | tf_op args[0]
  3.3 1.1 copy.13
  4.3 13.9 %collective-permute-start = (bf16[768,3,3,128]{3,0,2,1:T(8,128)(2,1)S(1)}, bf16[768,3,3,128]{3,0,2,1:T(8,128)(2,1)}, u32[]{:S(2)}, u32[]{:S(2)}) collective-permute-start(bf16[768,3,3,128]{3,0,2,1:T(8,128)(2,1)S(1)} %copy.13), channel_id=1, source_target_pairs={{0,32},{32,64},{64,96},{96,128},{128,160},{160,192},{192,224},{224... | collective-permute-start | bytes 5308424 | tf_op jit(solution)/shard_map/ppermute | solution.py:14
  18.2 1.3 copy.16
  19.5 0.2 iota_compare_fusion
  19.7 54.7 %collective-permute-done = bf16[768,3,3,128]{3,0,2,1:T(8,128)(2,1)} collective-permute-done((bf16[768,3,3,128]{3,0,2,1:T(8,128)(2,1)S(1)}, bf16[768,3,3,128]{3,0,2,1:T(8,128)(2,1)}, u32[]{:S(2)}, u32[]{:S(2)}) %collective-permute-start) | collective-permute-done | bytes 1769504 | tf_op jit(solution)/shard_map/ppermute | solution.py:14
  74.4 6.6 %fusion.16 = (f32[3,768]{1,0:T(4,128)S(1)}, f32[3,768,768]{1,2,0:T(8,128)}) fusion(pred[768,768]{0,1:T(8,128)(4,1)S(1)} %iota_compare_fusion, bf16[768,3,3,128]{3,0,2,1:T(8,128)(2,1)} %collective-permute-done), kind=kOutput, calls=%fused_computation.29 | convolution fusion | flops 460063488 | bytes 8856576 | tf_op jit(solution)/shard_map/sub | solution.py:33
  80.9 0.0 slice-start
  80.9 3.7 %fusion.7 = bf16[3,768,768]{1,2,0:T(8,128)(2,1)S(1)} fusion(f32[3,768,768]{1,2,0:T(8,128)} %get-tuple-element.7, f32[3,768]{1,0:T(4,128)S(1)} %get-tuple-element.6), kind=kLoop, calls=%fused_computation.10 | loop fusion | flops 3538944 | bytes 10626048 | tf_op jit(solution)/shard_map/convert_element_type | solution.py:35
  84.7 0.0 slice-start.1
  84.7 1.1 fusion.10
  85.8 2.7 %multiply_reduce_fusion = (f32[768,3]{0,1:T(4,128)S(1)}, bf16[3,768,128]{1,2,0:T(8,128)(2,1)}) fusion(bf16[768,3,128]{0,2,1:T(8,128)(2,1)S(1)} %bitcast.62, bf16[3,768,768]{1,2,0:T(8,128)(2,1)S(1)} %fusion.7, bf16[768,3,3,128]{3,0,2,1:T(8,128)(2,1)} %collective-permute-done), kind=kOutput, calls=%fused_computation.22 | convolution fusion | flops 454457088 | bytes 5317632 | tf_op jit(solution)/shard_map/hqk,khd->qhd/dot_general | solution.py:36
  88.5 0.0 slice-done
  88.5 0.0 slice-done.1
  88.5 2.2 %multiply_convert_fusion = bf16[3,768,768]{1,2,0:T(8,128)(2,1)S(1)} fusion(f32[3,768]{1,0:T(4,128)S(1)} %bitcast.64, f32[3,768,768]{1,2,0:T(8,128)S(1)} %bitcast.59, f32[3,768]{1,0:T(4,128)S(1)} %get-tuple-element.6, bf16[768,3,128]{0,2,1:T(8,128)(2,1)S(1)} %bitcast.63, bf16[768,3,3,128]{3,0,2,1:T(8,128)(2,1)} %collective-permute-done), kind=kOutput, calls=%fused_computation.1 | convolution fusion | flops 460062720 | bytes 11814912 | tf_op jit(solution)/shard_map/qhd,khd->hqk/dot_general | solution.py:42
  90.7 2.2 %fusion.11 = bf16[768,1,3,128]{3,0,2,1:T(8,128)(2,1)S(1)} fusion(bf16[3,768,768]{1,2,0:T(8,128)(2,1)S(1)} %multiply_convert_fusion, bf16[768,3,3,128]{3,0,2,1:T(8,128)(2,1)} %collective-permute-done), kind=kOutput, calls=%fused_computation.20 | convolution fusion | flops 453574656 | bytes 4718592 | tf_op jit(solution)/shard_map/hqk,qhd->khd/dot_general | solution.py:49
  92.8 2.5 %fusion.12 = bf16[768,1,3,128]{3,0,2,1:T(8,128)(2,1)S(1)} fusion(bf16[3,768,768]{1,2,0:T(8,128)(2,1)S(1)} %multiply_convert_fusion, bf16[768,3,3,128]{3,0,2,1:T(8,128)(2,1)} %collective-permute-done), kind=kOutput, calls=%fused_computation.21 | convolution fusion | flops 453574656 | bytes 4718592 | tf_op jit(solution)/shard_map/hqk,khd->qhd/dot_general | solution.py:46
  95.3 0.2 pad_maximum_fusion
  95.5 1.9 collective-permute-start.1
  97.4 2.1 %copy.22 = bf16[1,768,384]{2,1,0:T(8,128)(2,1)} copy(bf16[1,768,384]{1,2,0:T(8,128)(2,1)} %bitcast.60) | data formatting | bytes 1179648
  99.6 105.5 %collective-permute-done.1 = bf16[768,3,3,128]{3,0,2,1:T(8,128)(2,1)S(1)} collective-permute-done((bf16[768,3,3,128]{3,0,2,1:T(8,128)(2,1)S(1)}, bf16[768,3,3,128]{3,0,2,1:T(8,128)(2,1)S(1)}, u32[]{:S(2)}, u32[]{:S(2)}) %collective-permute-start.1) | collective-permute-done | bytes 1769504 | tf_op jit(solution)/shard_map/ppermute | solution.py:14
  205.0 0.9 copy.21
  205.9 2.2 %copy.23 = bf16[1,768,3,384]{3,1,2,0:T(8,128)(2,1)} copy(bf16[1,768,3,384]{1,3,2,0:T(8,128)(2,1)S(1)} %bitcast.56) | data formatting | bytes 3538944
  (1 shorter events, 0.0 us)
Async XLA Ops:
  4.3 70.0 %collective-permute-start = (bf16[768,3,3,128]{3,0,2,1:T(8,128)(2,1)S(1)}, bf16[768,3,3,128]{3,0,2,1:T(8,128)(2,1)}, u32[]{:S(2)}, u32[]{:S(2)}) collective-permute-start(bf16[768,3,3,128]{3,0,2,1:T(8,128)(2,1)S(1)} %copy.13), channel_id=1, source_target_pairs={{0,32},{32,64},{64,96},{96,128},{128,160},{160,192},{192,224},{224... | collective-permute-start | bytes 5308424 | tf_op jit(solution)/shard_map/ppermute | solution.py:14
  80.9 7.6 %slice-start = ((s8[7077888]{0:T(1024)(128)(4,1)}), s8[2883584]{0:T(1024)(128)(4,1)S(1)}, s32[]{:S(2)}) async-start(s8[7077888]{0:T(1024)(128)(4,1)} %bitcast.58), calls=%async_computation | async-start | bytes 5767168
  84.7 3.8 %slice-start.1 = ((s8[7077888]{0:T(1024)(128)(4,1)}), s8[4194304]{0:T(1024)(128)(4,1)S(1)}, s32[]{:S(2)}) async-start(s8[7077888]{0:T(1024)(128)(4,1)} %bitcast.58), calls=%async_computation.1 | async-start | bytes 8388608
  95.5 109.5 %collective-permute-start.1 = (bf16[768,3,3,128]{3,0,2,1:T(8,128)(2,1)S(1)}, bf16[768,3,3,128]{3,0,2,1:T(8,128)(2,1)S(1)}, u32[]{:S(2)}, u32[]{:S(2)}) collective-permute-start(bf16[768,3,3,128]{3,0,2,1:T(8,128)(2,1)S(1)} %pad_maximum_fusion), channel_id=1, source_target_pairs={{0,480},{32,0},{64,32},{96,64},{128,96},{160,128},{192,160},{224,1... | collective-permute-start | bytes 5308424 | tf_op jit(solution)/shard_map/ppermute | solution.py:14
where the time goes:
time: 209 us; the launch traced here: 208 us
  waiting for transfers between devices  160 us (77%)
  matrix products  17.1 us (8%)
  starting transfers between devices  15.8 us (8%)
  local copies, waits for them, and re-layouts  10.2 us (5%)
  other arithmetic  4.11 us (2%)
    ppermute x2, waiting for transfers between devices, from_behind(): return lax.ppermute(value, axis, pairs)  160 us
    ppermute x2, starting transfers between devices, from_behind(): return lax.ppermute(value, axis, pairs)  15.8 us
    unnamed x8, local copies, waits for them, and re-layouts  8.27 us
    sub x1, matrix products, on_device(): expo = jnp.exp(scores - peak)  6.56 us
  transfers between devices with their start and end apart: 2, of which 2 were waited for; matrix products, arithmetic and copies ran while one was open for 2% of the time, Pallas kernels for 0%

commit v1 on v0

v1 whole, which is shorter than its diff:
```python
import math
import functools
import jax
import jax.numpy as jnp
from jax import lax
from jax.experimental import pallas as pl
from jax.experimental.pallas import tpu as pltpu
from jax.sharding import PartitionSpec as P

HD = 128
BLK = 256


def from_behind(value, axis, steps):
    count = lax.axis_size(axis)
    pairs = [(source, (source + steps) % count) for source in range(count)]
    return lax.ppermute(value, axis, pairs)


def dot_nt(a, b):
    return lax.dot_general(a, b, (((1,), (1,)), ((), ())), preferred_element_type=jnp.float32)


def dot_nn(a, b):
    return lax.dot_general(a, b, (((1,), (0,)), ((), ())), preferred_element_type=jnp.float32)


def dot_tn(a, b):
    return lax.dot_general(a, b, (((0,), (0,)), ((), ())), preferred_element_type=jnp.float32)


def probabilities(query, keys, first):
    scores = dot_nt(query, keys)
    rows = lax.broadcasted_iota(jnp.int32, scores.shape, 0) + first
    cols = lax.broadcasted_iota(jnp.int32, scores.shape, 1)
    scores = jnp.where(cols <= rows, scores, -jnp.inf)
    peak = jnp.max(scores, axis=1, keepdims=True)
    expo = jnp.exp2((scores - peak) * (math.log2(math.e) / math.sqrt(HD)))
    return expo * (1.0 / jnp.sum(expo, axis=1, keepdims=True))


def forward_kernel(qkv_ref, out_ref, weights_ref):
    length, width = out_ref.shape
    for head in range(width // HD):
        at = slice(head * HD, (head + 1) * HD)
        for first in range(0, length, BLK):
            q_at, k_at = slice(first, first + BLK), slice(0, first + BLK)
            probs = probabilities(qkv_ref[0, q_at, at], qkv_ref[1, k_at, at], first)
            weights = probs.astype(jnp.bfloat16)
            weights_ref[head, q_at, k_at] = weights
            out_ref[q_at, at] = dot_nn(weights, qkv_ref[2, k_at, at]).astype(jnp.bfloat16)


def backward_kernel(qkv_ref, weights_ref, out_ref, dout_ref, grads_ref):
    length, width = out_ref.shape
    scale = 1.0 / math.sqrt(HD)
    for head in range(width // HD):
        at = slice(head * HD, (head + 1) * HD)
        dk = [None] * (length // BLK)
        dv = [None] * (length // BLK)
        for i in range(length // BLK):
            q_at, k_at = slice(i * BLK, (i + 1) * BLK), slice(0, (i + 1) * BLK)
            dout = dout_ref[q_at, at]
            delta = jnp.sum(dout.astype(jnp.float32) * out_ref[q_at, at].astype(jnp.float32), axis=1, keepdims=True)
            weights = weights_ref[head, q_at, k_at]
            grad_p = dot_nt(dout, qkv_ref[2, k_at, at])
            grad_s = (weights.astype(jnp.float32) * (grad_p - delta)).astype(jnp.bfloat16)
            grads_ref[0, q_at, at] = (dot_nn(grad_s, qkv_ref[1, k_at, at]) * scale).astype(jnp.bfloat16)
            query = qkv_ref[0, q_at, at]
            for j in range(i + 1):
                sub = slice(j * BLK, (j + 1) * BLK)
                kk = dot_tn(grad_s[:, sub], query)
                vv = dot_tn(weights[:, sub], dout)
                dk[j] = kk if dk[j] is None else dk[j] + kk
                dv[j] = vv if dv[j] is None else dv[j] + vv
        for j in range(length // BLK):
            sub = slice(j * BLK, (j + 1) * BLK)
            grads_ref[1, sub, at] = (dk[j] * scale).astype(jnp.bfloat16)
            grads_ref[2, sub, at] = dv[j].astype(jnp.bfloat16)


VMEM = pl.BlockSpec(memory_space=pltpu.VMEM)


def forward(qkv):
    _, length, width = qkv.shape
    heads = width // HD
    return pl.pallas_call(
        forward_kernel,
        out_shape=(
            jax.ShapeDtypeStruct((length, width), jnp.bfloat16),
            jax.ShapeDtypeStruct((heads, length, length), jnp.bfloat16),
        ),
        in_specs=[VMEM],
        out_specs=(VMEM, VMEM),
        name="forward",
        compiler_params=pltpu.CompilerParams(vmem_limit_bytes=24 * 2**20),
        cost_estimate=pl.CostEstimate(
            flops=4 * heads * length * length * HD, bytes_accessed=4 * length * width * 2, transcendentals=heads * length * length
        ),
    )(qkv)


def backward(qkv, weights, out, dout):
    _, length, width = qkv.shape
    heads = width // HD
    return pl.pallas_call(
        backward_kernel,
        out_shape=jax.ShapeDtypeStruct(qkv.shape, jnp.bfloat16),
        in_specs=[VMEM] * 4,
        out_specs=VMEM,
        name="backward",
        compiler_params=pltpu.CompilerParams(vmem_limit_bytes=24 * 2**20),
        cost_estimate=pl.CostEstimate(
            flops=8 * heads * length * length * HD, bytes_accessed=9 * length * width * 2, transcendentals=0
        ),
    )(qkv, weights, out, dout)


def on_device(qkv_sent, grad_out):
    qkv = qkv_sent[0].transpose(1, 0, 2)
    dout = from_behind(grad_out[0], "section", -1)
    out, weights = forward(qkv)
    attn_out = from_behind(out, "section", 1)
    grads = backward(qkv, weights, out, dout)
    return (attn_out[None], grads.transpose(1, 0, 2)[None])


def solution(mesh):
    in_specs = (P("section", None, None, "tp"), P("section", None, "tp"))
    out_specs = (P("section", None, "tp"), P("section", None, None, "tp"))
    return jax.shard_map(
        on_device, mesh=mesh, in_specs=in_specs, out_specs=out_specs, check_vma=False
    )
```

time: 209 us -> 67.1 us (0.32)
  the two profiles are of different devices: /device:TPU:89 before, /device:TPU:63 now
where the time goes in v1:
time: 67.1 us; the launch traced here: 66.9 us
  waiting for transfers between devices  38.6 us (58%)
  starting transfers between devices  16.7 us (25%)
  Pallas kernels  8.61 us (13%)
  local copies, waits for them, and re-layouts  2.29 us (3%)
    ppermute x2, waiting for transfers between devices, from_behind(): return lax.ppermute(value, axis, pairs)  38.6 us
    ppermute x2, starting transfers between devices, from_behind(): return lax.ppermute(value, axis, pairs)  16.7 us
    pallas_call x1, Pallas kernels, backward(): pl.pallas_call(backward_kernel, out_shape=jax.ShapeDtypeStruct(qkv.shape,...  4.44 us
    pallas_call x1, Pallas kernels, forward(): pl.pallas_call(forward_kernel, out_shape=(jax.ShapeDtypeStruct((length, w...  4.17 us
    unnamed x5, local copies, waits for them, and re-layouts  2.29 us
  transfers between devices with their start and end apart: 2, of which 2 were waited for; matrix products, arithmetic and copies ran while one was open for 0% of the time, Pallas kernels for 0%

profile of v1, /device:TPU:63, one launch (start us, length us, event | category | flops | bytes accessed | tf_op | source)
XLA Modules:
  0.0 66.9 jit_solution(9682428229004639419)
XLA Ops:
  0.6 0.0 copy-start
  0.6 1.5 %copy-done = bf16[1,768,3,384]{3,1,2,0:T(8,128)(2,1)S(1)} copy-done((bf16[1,768,3,384]{3,1,2,0:T(8,128)(2,1)S(1)}, bf16[1,768,3,384]{3,1,2,0:T(8,128)(2,1)}, u32[]{:S(2)}) %copy-start) | copy-done | bytes 1769496
  2.1 0.0 copy-start.1
  2.1 4.2 %forward.1 = (bf16[768,384]{1,0:T(8,128)(2,1)S(1)}, bf16[3,768,768]{2,1,0:T(8,128)(2,1)S(1)}) custom-call(bf16[3,768,384]{2,1,0:T(8,128)(2,1)S(1)} %bitcast.8), custom_call_target="tpu_custom_call" | custom-call | flops 905969664 | bytes 2359296 | tf_op jit(solution)/shard_map/forward/pallas_call | solution.py:88
  6.3 14.8 %collective-permute-start = (bf16[768,384]{1,0:T(8,128)(2,1)S(1)}, bf16[768,384]{1,0:T(8,128)(2,1)S(1)}, u32[]{:S(2)}, u32[]{:S(2)}) collective-permute-start(bf16[768,384]{1,0:T(8,128)(2,1)S(1)} %get-tuple-element.4.out_ref), channel_id=1, source_target_pairs={{0,32},{32,64},{64,96},{96,128},{128,160},{160,192},{192,224},{224... | collective-permute-start | bytes 1769480 | tf_op jit(solution)/shard_map/ppermute | solution.py:17
  21.1 0.0 copy-done.1
  21.1 1.9 %collective-permute-start.1 = (bf16[768,384]{1,0:T(8,128)(2,1)S(1)}, bf16[768,384]{1,0:T(8,128)(2,1)S(1)}, u32[]{:S(2)}, u32[]{:S(2)}) collective-permute-start(bf16[768,384]{1,0:T(8,128)(2,1)S(1)} %bitcast.12), channel_id=1, source_target_pairs={{0,480},{32,0},{64,32},{96,64},{128,96},{160,128},{192,160},{224,1... | collective-permute-start | bytes 1769480 | tf_op jit(solution)/shard_map/ppermute | solution.py:17
  23.0 23.1 %collective-permute-done = bf16[768,384]{1,0:T(8,128)(2,1)S(1)} collective-permute-done((bf16[768,384]{1,0:T(8,128)(2,1)S(1)}, bf16[768,384]{1,0:T(8,128)(2,1)S(1)}, u32[]{:S(2)}, u32[]{:S(2)}) %collective-permute-start) | collective-permute-done | bytes 589856 | tf_op jit(solution)/shard_map/ppermute | solution.py:17
  46.1 15.5 %collective-permute-done.1.dout_ref = bf16[768,384]{1,0:T(8,128)(2,1)S(1)} collective-permute-done((bf16[768,384]{1,0:T(8,128)(2,1)S(1)}, bf16[768,384]{1,0:T(8,128)(2,1)S(1)}, u32[]{:S(2)}, u32[]{:S(2)}) %collective-permute-start.1) | collective-permute-done | bytes 589856 | tf_op jit(solution)/shard_map/ppermute | solution.py:17
  61.6 4.4 %backward.1 = bf16[3,768,384]{2,1,0:T(8,128)(2,1)} custom-call(bf16[3,768,384]{2,1,0:T(8,128)(2,1)S(1)} %bitcast.9, bf16[3,768,768]{2,1,0:T(8,128)(2,1)S(1)} %get-tuple-element.5.weights_ref, bf16[768,384]{1,0:T(8,128)(2,1)S(1)} %get-tuple-element.4.out_ref, bf16[768,384]{1,0:T(8,128)(2,1)S(1)} %collective-permute-done.1.dout_ref), custom_call_target="tpu_custom_call" | custom-call | flops 1811939328 | bytes 5308416 | tf_op jit(solution)/shard_map/backward/pallas_call | solution.py:107
  66.1 0.8 %copy.5 = bf16[1,768,384]{2,1,0:T(8,128)(2,1)} copy(bf16[1,768,384]{2,1,0:T(8,128)(2,1)S(1)} %bitcast.11) | data formatting | bytes 1179648
Async XLA Ops:
  0.6 1.5 %copy-start = (bf16[1,768,3,384]{3,1,2,0:T(8,128)(2,1)S(1)}, bf16[1,768,3,384]{3,1,2,0:T(8,128)(2,1)}, u32[]{:S(2)}) copy-start(bf16[1,768,3,384]{3,1,2,0:T(8,128)(2,1)} %param.2) | copy-start | bytes 5308420
  2.1 19.0 %copy-start.1 = (bf16[1,768,384]{2,1,0:T(8,128)(2,1)S(1)}, bf16[1,768,384]{2,1,0:T(8,128)(2,1)}, u32[]{:S(2)}) copy-start(bf16[1,768,384]{2,1,0:T(8,128)(2,1)} %param.3) | copy-start | bytes 1769476
  6.3 39.8 %collective-permute-start = (bf16[768,384]{1,0:T(8,128)(2,1)S(1)}, bf16[768,384]{1,0:T(8,128)(2,1)S(1)}, u32[]{:S(2)}, u32[]{:S(2)}) collective-permute-start(bf16[768,384]{1,0:T(8,128)(2,1)S(1)} %get-tuple-element.4.out_ref), channel_id=1, source_target_pairs={{0,32},{32,64},{64,96},{96,128},{128,160},{160,192},{192,224},{224... | collective-permute-start | bytes 1769480 | tf_op jit(solution)/shard_map/ppermute | solution.py:17
  21.1 40.5 %collective-permute-start.1 = (bf16[768,384]{1,0:T(8,128)(2,1)S(1)}, bf16[768,384]{1,0:T(8,128)(2,1)S(1)}, u32[]{:S(2)}, u32[]{:S(2)}) collective-permute-start(bf16[768,384]{1,0:T(8,128)(2,1)S(1)} %bitcast.12), channel_id=1, source_target_pairs={{0,480},{32,0},{64,32},{96,64},{128,96},{160,128},{192,160},{224,1... | collective-permute-start | bytes 1769480 | tf_op jit(solution)/shard_map/ppermute | solution.py:17

commit v2 on v0

v2 whole, which is shorter than its diff:
```python
import math
import jax
import jax.numpy as jnp
from jax import lax
from jax.experimental import pallas as pl
from jax.experimental.pallas import tpu as pltpu
from jax.sharding import PartitionSpec as P

HD = 128
BLK = 256
SECTION = "section"
FACTOR = math.log2(math.e) / math.sqrt(HD)
SCALE = 1.0 / math.sqrt(HD)


def near_pairs(count, half, steps):
    pairs = [(source, (source + steps) % count) for source in range(count)]
    return [(source, target) for source, target in pairs if source // half == target // half]


def far_pairs(count, half, moves):
    return [
        (base + source, (base + half + target) % count)
        for base in range(0, count, half)
        for source, target in moves
    ]


def same_pairs(count, half, moves):
    return [(base + source, base + target) for base in range(0, count, half) for source, target in moves]


def dot_nt(a, b):
    return lax.dot_general(a, b, (((1,), (1,)), ((), ())), preferred_element_type=jnp.float32)


def dot_nn(a, b):
    return lax.dot_general(a, b, (((1,), (0,)), ((), ())), preferred_element_type=jnp.float32)


def dot_tn(a, b):
    return lax.dot_general(a, b, (((0,), (0,)), ((), ())), preferred_element_type=jnp.float32)


def lanes(head, wide=1):
    return slice(head * HD * wide, (head + 1) * HD * wide)


def forward_kernel(half, qkv_ref, dout_ref, out_ref, relay_ref, direct_ref, expo_ref, inverse_ref, values_ref):
    length, width = out_ref.shape
    heads = width // HD
    cut = relay_ref.shape[0]
    for head in range(heads):
        values_ref[:, 2 * head * HD : (2 * head + 1) * HD] = qkv_ref[2, :, lanes(head)]
        values_ref[:, (2 * head + 1) * HD : (2 * head + 2) * HD] = jnp.ones((length, HD), jnp.bfloat16)
    for first in range(0, length, BLK):
        q_at, k_at = slice(first, first + BLK), slice(0, first + BLK)
        for head in range(heads):
            at = lanes(head)
            scores = dot_nt(qkv_ref[0, q_at, at], qkv_ref[1, k_at, at])
            rows = lax.broadcasted_iota(jnp.int32, scores.shape, 0) + first
            cols = lax.broadcasted_iota(jnp.int32, scores.shape, 1)
            scores = jnp.where(cols <= rows, scores, -jnp.inf)
            peak = jnp.max(scores, axis=1, keepdims=True)
            expo = jnp.exp2((scores - peak) * FACTOR).astype(jnp.bfloat16)
            expo_ref[head, q_at, k_at] = expo
            both = dot_nn(expo, values_ref[k_at, lanes(head, 2)])
            inverse = 1.0 / both[:, HD:]
            inverse_ref[q_at, at] = inverse
            out_ref[q_at, at] = (both[:, :HD] * inverse).astype(jnp.bfloat16)
    sends_dout = lax.rem(lax.axis_index(SECTION), half) == 0

    @pl.when(sends_dout)
    def _():
        relay_ref[...] = dout_ref[0:cut]
        direct_ref[...] = dout_ref[cut:length]

    @pl.when(jnp.logical_not(sends_dout))
    def _():
        relay_ref[...] = out_ref[0:cut]
        direct_ref[...] = out_ref[cut:length]


def backward_kernel(
    half,
    qkv_ref,
    expo_ref,
    inverse_ref,
    values_ref,
    out_ref,
    near_dout_ref,
    near_out_ref,
    relay_ref,
    direct_ref,
    attn_ref,
    grads_ref,
    dout_ref,
    stage_ref,
    attn_sem,
    grads_sem,
):
    length, width = out_ref.shape
    heads = width // HD
    cut = relay_ref.shape[0]
    place = lax.rem(lax.axis_index(SECTION), half)
    parts = ((0, cut, relay_ref), (cut, length, direct_ref))

    def send(source, k, start, stop):
        return pltpu.make_async_copy(source, attn_ref.at[start:stop], attn_sem.at[k])

    @pl.when(place == 0)
    def _():
        for k, (start, stop, ref) in enumerate(parts):
            send(ref, k, start, stop).start()

    @pl.when(place != 0)
    def _():
        for k, (start, stop, _) in enumerate(parts):
            send(near_out_ref.at[start:stop], k, start, stop).start()

    def prepare(start, stop, dout):
        for head in range(heads):
            at = lanes(head)
            scaled = dout[:, at].astype(jnp.float32) * inverse_ref[start:stop, at]
            dout_ref[start:stop, 2 * head * HD : (2 * head + 1) * HD] = scaled.astype(jnp.bfloat16)
            product = scaled * out_ref[start:stop, at].astype(jnp.float32)
            dout_ref[start:stop, (2 * head + 1) * HD : (2 * head + 2) * HD] = (-product).astype(jnp.bfloat16)

    @pl.when(place == half - 1)
    def _():
        for start, stop, ref in parts:
            prepare(start, stop, ref)

    @pl.when(place != half - 1)
    def _():
        prepare(0, length, near_dout_ref)

    n = length // BLK
    copies = []
    for head in range(heads):
        at, wide = lanes(head), lanes(head, 2)
        dk, dv = [None] * n, [None] * n
        for i in range(n):
            q_at, k_at = slice(i * BLK, (i + 1) * BLK), slice(0, (i + 1) * BLK)
            expo = expo_ref[head, q_at, k_at]
            grad_p = dot_nt(dout_ref[q_at, wide], values_ref[k_at, wide])
            grad_s = (expo.astype(jnp.float32) * grad_p).astype(jnp.bfloat16)
            stage_ref[0, q_at, at] = (dot_nn(grad_s, qkv_ref[1, k_at, at]) * SCALE).astype(jnp.bfloat16)
            for j in range(i + 1):
                sub = slice(j * BLK, (j + 1) * BLK)
                kk = dot_tn(grad_s[:, sub], qkv_ref[0, q_at, at])
                vv = dot_tn(expo[:, sub], dout_ref[q_at, 2 * head * HD : (2 * head + 1) * HD])
                dk[j] = kk if dk[j] is None else dk[j] + kk
                dv[j] = vv if dv[j] is None else dv[j] + vv
        for j in range(n):
            sub = slice(j * BLK, (j + 1) * BLK)
            stage_ref[1, sub, at] = (dk[j] * SCALE).astype(jnp.bfloat16)
            stage_ref[2, sub, at] = dv[j].astype(jnp.bfloat16)
        copy = pltpu.make_async_copy(stage_ref.at[:, :, at], grads_ref.at[:, :, at], grads_sem.at[head])
        copy.start()
        copies.append(copy)
    for copy in copies:
        copy.wait()
    for k, (start, stop, _) in enumerate(parts):
        send(near_out_ref.at[start:stop], k, start, stop).wait()


VMEM = pl.BlockSpec(memory_space=pltpu.VMEM)
ANY = pl.BlockSpec(memory_space=pl.ANY)


def on_device(qkv_sent, grad_out):
    bf16 = jnp.bfloat16
    qkv = qkv_sent[0].transpose(1, 0, 2)
    dout = grad_out[0]
    _, length, width = qkv.shape
    heads = width // HD
    cut = length // 2
    count = lax.axis_size(SECTION)
    half = count // 2
    last = half - 1
    work = heads * length * length * HD
    struct = jax.ShapeDtypeStruct
    params = pltpu.CompilerParams(vmem_limit_bytes=28 * 2**20)

    near_dout = lax.ppermute(dout, SECTION, near_pairs(count, half, -1))
    out, relay, direct, expo, inverse, values = pl.pallas_call(
        lambda *refs: forward_kernel(half, *refs),
        out_shape=(
            struct((length, width), bf16),
            struct((cut, width), bf16),
            struct((length - cut, width), bf16),
            struct((heads, length, length), bf16),
            struct((length, width), jnp.float32),
            struct((length, 2 * width), bf16),
        ),
        in_specs=[VMEM] * 2,
        out_specs=(VMEM,) * 6,
        name="forward",
        compiler_params=params,
        cost_estimate=pl.CostEstimate(flops=4 * work, bytes_accessed=12 * length * width, transcendentals=0),
    )(qkv, dout)
    relay = lax.ppermute(relay, SECTION, same_pairs(count, half, [(0, 2), (last, last - 2)]))
    near_out = lax.ppermute(out, SECTION, near_pairs(count, half, 1))
    relay, direct = lax.optimization_barrier((relay, direct))
    relay = lax.ppermute(relay, SECTION, far_pairs(count, half, [(2, last), (last - 2, 0)]))
    direct = lax.ppermute(direct, SECTION, far_pairs(count, half, [(0, last), (last, 0)]))
    attn_out, grads = pl.pallas_call(
        lambda *refs: backward_kernel(half, *refs),
        out_shape=(struct((length, width), bf16), struct(qkv.shape, bf16)),
        in_specs=[VMEM] * 5 + [VMEM] * 4,
        out_specs=(ANY, ANY),
        scratch_shapes=[
            pltpu.VMEM((length, 2 * width), bf16),
            pltpu.VMEM(qkv.shape, bf16),
            pltpu.SemaphoreType.DMA((2,)),
            pltpu.SemaphoreType.DMA((heads,)),
        ],
        name="backward",
        compiler_params=params,
        cost_estimate=pl.CostEstimate(flops=8 * work, bytes_accessed=18 * length * width, transcendentals=0),
    )(qkv, expo, inverse, values, out, near_dout, near_out, relay, direct)
    return (attn_out[None], grads.transpose(1, 0, 2)[None])


def solution(mesh):
    in_specs = (P("section", None, None, "tp"), P("section", None, "tp"))
    out_specs = (P("section", None, "tp"), P("section", None, None, "tp"))
    return jax.shard_map(
        on_device, mesh=mesh, in_specs=in_specs, out_specs=out_specs, check_vma=False
    )
```

time: 209 us -> 50.4 us (0.24)
  the two profiles are of different devices: /device:TPU:89 before, /device:TPU:38 now
where the time goes in v2:
time: 50.4 us; the launch traced here: 50.1 us
  starting transfers between devices  25.2 us (50%)
  waiting for transfers between devices  14.9 us (30%)
  Pallas kernels  6.77 us (13%)
  local copies, waits for them, and re-layouts  2.54 us (5%)
  between operations  0.71 us (1%)
    ppermute x1, starting transfers between devices, on_device(): lax.ppermute(direct, SECTION, far_pairs(count, half, [(0, last), (last, 0...  16 us
    ppermute x1, waiting for transfers between devices, on_device(): lax.ppermute(relay, SECTION, far_pairs(count, half, [(2, last), (last - 2...  14.7 us
    pallas_call x1, Pallas kernels, on_device(): pl.pallas_call(lambda *refs: backward_kernel(half, *refs), out_shape=(str...  4.44 us
    ppermute x1, starting transfers between devices, on_device(): lax.ppermute(relay, SECTION, same_pairs(count, half, [(0, 2), (last, last...  3.51 us
    ppermute x1, starting transfers between devices, on_device(): near_out = lax.ppermute(out, SECTION, near_pairs(count, half, 1))  3.07 us
    unnamed x6, local copies, waits for them, and re-layouts  2.54 us
    pallas_call x1, Pallas kernels, on_device(): pl.pallas_call(lambda *refs: forward_kernel(half, *refs), out_shape=(stru...  2.33 us
    ppermute x1, starting transfers between devices, on_device(): near_dout = lax.ppermute(dout, SECTION, near_pairs(count, half, -1))  1.29 us
  transfers between devices with their start and end apart: 5, of which 2 were waited for; matrix products, arithmetic and copies ran while one was open for 0% of the time, Pallas kernels for 0%

profile of v2, /device:TPU:38, one launch (start us, length us, event | category | flops | bytes accessed | tf_op | source)
XLA Modules:
  0.0 50.1 jit_solution(1038009085742828645)
XLA Ops:
  0.6 0.0 copy-start
  0.6 1.5 %copy-done = bf16[1,768,3,384]{3,1,2,0:T(8,128)(2,1)S(1)} copy-done((bf16[1,768,3,384]{3,1,2,0:T(8,128)(2,1)S(1)}, bf16[1,768,3,384]{3,1,2,0:T(8,128)(2,1)}, u32[]{:S(2)}) %copy-start) | copy-done | bytes 1769496
  2.1 0.0 copy-start.1
  2.1 1.1 %copy-done.1 = bf16[1,768,384]{2,1,0:T(8,128)(2,1)S(1)} copy-done((bf16[1,768,384]{2,1,0:T(8,128)(2,1)S(1)}, bf16[1,768,384]{2,1,0:T(8,128)(2,1)}, u32[]{:S(2)}) %copy-start.1) | copy-done | bytes 589848
  3.2 0.0 copy-start.2
  3.2 2.3 %forward.1 = (bf16[768,384]{1,0:T(8,128)(2,1)S(1)}, bf16[384,384]{1,0:T(8,128)(2,1)S(1)}, bf16[384,384]{1,0:T(8,128)(2,1)S(1)}, bf16[3,768,768]{2,1,0:T(8,128)(2...) custom-call(bf16[3,768,384]{2,1,0:T(8,128)(2,1)S(1)} %bitcast.8, bf16[768,384]{1,0:T(8,128)(2,1)S(1)} %bitcast.10), custom_call_target="tpu_custom_call" | custom-call | flops 905969664 | bytes 3538944 | tf_op jit(solution)/shard_map/forward/pallas_call | solution.py:187
  5.5 3.5 %collective-permute-start.2 = (bf16[384,384]{1,0:T(8,128)(2,1)S(1)}, bf16[384,384]{1,0:T(8,128)(2,1)S(1)}, u32[]{:S(2)}, u32[]{:S(2)}) collective-permute-start(bf16[384,384]{1,0:T(8,128)(2,1)S(1)} %get-tuple-element.16), channel_id=1, source_target_pairs={{0,64},{224,160},{256,320},{480,416},{1,65},{225,161},{257,321},{4... | collective-permute-start | bytes 884744 | tf_op jit(solution)/shard_map/ppermute | solution.py:203
  9.0 0.0 copy-done.2
  9.0 1.3 %collective-permute-start = (bf16[768,384]{1,0:T(8,128)(2,1)S(1)}, bf16[768,384]{1,0:T(8,128)(2,1)S(1)}, u32[]{:S(2)}, u32[]{:S(2)}) collective-permute-start(bf16[768,384]{1,0:T(8,128)(2,1)S(1)} %bitcast.11), channel_id=1, source_target_pairs={{32,0},{64,32},{96,64},{128,96},{160,128},{192,160},{224,192},{288... | collective-permute-start | bytes 1769480 | tf_op jit(solution)/shard_map/ppermute | solution.py:186
  10.3 3.1 %collective-permute-start.1 = (bf16[768,384]{1,0:T(8,128)(2,1)S(1)}, bf16[768,384]{1,0:T(8,128)(2,1)S(1)}, u32[]{:S(2)}, u32[]{:S(2)}) collective-permute-start(bf16[768,384]{1,0:T(8,128)(2,1)S(1)} %get-tuple-element.15.refs_4_), channel_id=1, source_target_pairs={{0,32},{32,64},{64,96},{96,128},{128,160},{160,192},{192,224},{256... | collective-permute-start | bytes 1769480 | tf_op jit(solution)/shard_map/ppermute | solution.py:204
  13.4 0.0 collective-permute-done.2
  13.4 1.3 %collective-permute-start.3 = (bf16[384,384]{1,0:T(8,128)(2,1)S(1)}, bf16[384,384]{1,0:T(8,128)(2,1)S(1)}, u32[]{:S(2)}, u32[]{:S(2)}) collective-permute-start(bf16[384,384]{1,0:T(8,128)(2,1)S(1)} %collective-permute-done.2), channel_id=1, source_target_pairs={{64,480},{160,256},{320,224},{416,0},{65,481},{161,257},{321,225},... | collective-permute-start | bytes 884744 | tf_op jit(solution)/shard_map/ppermute | solution.py:206
  14.7 16.0 %collective-permute-start.4 = (bf16[384,384]{1,0:T(8,128)(2,1)S(1)}, bf16[384,384]{1,0:T(8,128)(2,1)S(1)}, u32[]{:S(2)}, u32[]{:S(2)}) collective-permute-start(bf16[384,384]{1,0:T(8,128)(2,1)S(1)} %get-tuple-element.19), channel_id=1, source_target_pairs={{0,480},{224,256},{256,224},{480,0},{1,481},{225,257},{257,225},{4... | collective-permute-start | bytes 884744 | tf_op jit(solution)/shard_map/ppermute | solution.py:207
  30.8 0.0 collective-permute-done.refs_5_
  30.8 14.7 %collective-permute-done.3.refs_7_ = bf16[384,384]{1,0:T(8,128)(2,1)S(1)} collective-permute-done((bf16[384,384]{1,0:T(8,128)(2,1)S(1)}, bf16[384,384]{1,0:T(8,128)(2,1)S(1)}, u32[]{:S(2)}, u32[]{:S(2)}) %collective-permute-start.3) | collective-permute-done | bytes 294944 | tf_op jit(solution)/shard_map/ppermute | solution.py:206
  45.5 0.2 collective-permute-done.4.refs_8_
  45.7 0.0 collective-permute-done.1.refs_6_
  45.7 4.4 %backward.1 = (bf16[768,384]{1,0:T(8,128)(2,1)}, bf16[3,768,384]{2,1,0:T(8,128)(2,1)}) custom-call(bf16[3,768,384]{2,1,0:T(8,128)(2,1)S(1)} %bitcast.9, bf16[3,768,768]{2,1,0:T(8,128)(2,1)S(1)} %get-tuple-element.12.refs_1_, f32[768,384]{1,0:T(8,128)S(1)} %get-tuple-element.13.refs_2_, bf16[768,768]{1,0:T(8,128)(2,1)S(1)} %get-tuple-element.14.refs_3_, ...), custom_call_target="tpu_custom_call" | custom-call | flops 1811939328 | bytes 5308416 | tf_op jit(solution)/shard_map/backward/pallas_call | solution.py:208
Async XLA Ops:
  0.6 1.5 %copy-start = (bf16[1,768,3,384]{3,1,2,0:T(8,128)(2,1)S(1)}, bf16[1,768,3,384]{3,1,2,0:T(8,128)(2,1)}, u32[]{:S(2)}) copy-start(bf16[1,768,3,384]{3,1,2,0:T(8,128)(2,1)} %param.2) | copy-start | bytes 5308420
  2.1 1.1 %copy-start.1 = (bf16[1,768,384]{2,1,0:T(8,128)(2,1)S(1)}, bf16[1,768,384]{2,1,0:T(8,128)(2,1)}, u32[]{:S(2)}) copy-start(bf16[1,768,384]{2,1,0:T(8,128)(2,1)} %param.3) | copy-start | bytes 1769476
  3.2 5.9 %copy-start.2 = (bf16[1,768,384]{2,1,0:T(8,128)(2,1)S(1)}, bf16[1,768,384]{2,1,0:T(8,128)(2,1)}, u32[]{:S(2)}) copy-start(bf16[1,768,384]{2,1,0:T(8,128)(2,1)} %param.3) | copy-start | bytes 1769476
  5.5 7.9 %collective-permute-start.2 = (bf16[384,384]{1,0:T(8,128)(2,1)S(1)}, bf16[384,384]{1,0:T(8,128)(2,1)S(1)}, u32[]{:S(2)}, u32[]{:S(2)}) collective-permute-start(bf16[384,384]{1,0:T(8,128)(2,1)S(1)} %get-tuple-element.16), channel_id=1, source_target_pairs={{0,64},{224,160},{256,320},{480,416},{1,65},{225,161},{257,321},{4... | collective-permute-start | bytes 884744 | tf_op jit(solution)/shard_map/ppermute | solution.py:203
  9.0 21.7 %collective-permute-start = (bf16[768,384]{1,0:T(8,128)(2,1)S(1)}, bf16[768,384]{1,0:T(8,128)(2,1)S(1)}, u32[]{:S(2)}, u32[]{:S(2)}) collective-permute-start(bf16[768,384]{1,0:T(8,128)(2,1)S(1)} %bitcast.11), channel_id=1, source_target_pairs={{32,0},{64,32},{96,64},{128,96},{160,128},{192,160},{224,192},{288... | collective-permute-start | bytes 1769480 | tf_op jit(solution)/shard_map/ppermute | solution.py:186
  10.3 35.3 %collective-permute-start.1 = (bf16[768,384]{1,0:T(8,128)(2,1)S(1)}, bf16[768,384]{1,0:T(8,128)(2,1)S(1)}, u32[]{:S(2)}, u32[]{:S(2)}) collective-permute-start(bf16[768,384]{1,0:T(8,128)(2,1)S(1)} %get-tuple-element.15.refs_4_), channel_id=1, source_target_pairs={{0,32},{32,64},{64,96},{96,128},{128,160},{160,192},{192,224},{256... | collective-permute-start | bytes 1769480 | tf_op jit(solution)/shard_map/ppermute | solution.py:204
  13.4 32.1 %collective-permute-start.3 = (bf16[384,384]{1,0:T(8,128)(2,1)S(1)}, bf16[384,384]{1,0:T(8,128)(2,1)S(1)}, u32[]{:S(2)}, u32[]{:S(2)}) collective-permute-start(bf16[384,384]{1,0:T(8,128)(2,1)S(1)} %collective-permute-done.2), channel_id=1, source_target_pairs={{64,480},{160,256},{320,224},{416,0},{65,481},{161,257},{321,225},... | collective-permute-start | bytes 884744 | tf_op jit(solution)/shard_map/ppermute | solution.py:206
  14.7 30.9 %collective-permute-start.4 = (bf16[384,384]{1,0:T(8,128)(2,1)S(1)}, bf16[384,384]{1,0:T(8,128)(2,1)S(1)}, u32[]{:S(2)}, u32[]{:S(2)}) collective-permute-start(bf16[384,384]{1,0:T(8,128)(2,1)S(1)} %get-tuple-element.19), channel_id=1, source_target_pairs={{0,480},{224,256},{256,224},{480,0},{1,481},{225,257},{257,225},{4... | collective-permute-start | bytes 884744 | tf_op jit(solution)/shard_map/ppermute | solution.py:207

commit v3 on v2

v3 whole, which is shorter than its diff:
```python
import math
import jax
import jax.numpy as jnp
from jax import lax
from jax.experimental import pallas as pl
from jax.experimental.pallas import tpu as pltpu
from jax.sharding import PartitionSpec as P

HD = 128
BLK = 256
SECTION = "section"
FACTOR = math.log2(math.e) / math.sqrt(HD)
SCALE = 1.0 / math.sqrt(HD)


def near_pairs(count, half, steps):
    pairs = [(source, (source + steps) % count) for source in range(count)]
    return [(source, target) for source, target in pairs if source // half == target // half]


def far_pairs(count, half, moves):
    return [
        (base + source, (base + half + target) % count)
        for base in range(0, count, half)
        for source, target in moves
    ]


def same_pairs(count, half, moves):
    return [(base + source, base + target) for base in range(0, count, half) for source, target in moves]


def dot_nt(a, b):
    return lax.dot_general(a, b, (((1,), (1,)), ((), ())), preferred_element_type=jnp.float32)


def dot_nn(a, b):
    return lax.dot_general(a, b, (((1,), (0,)), ((), ())), preferred_element_type=jnp.float32)


def dot_tn(a, b):
    return lax.dot_general(a, b, (((0,), (0,)), ((), ())), preferred_element_type=jnp.float32)


def lanes(head, wide=1):
    return slice(head * HD * wide, (head + 1) * HD * wide)


def attend(qkv_ref, values_ref, expo_ref, inverse_ref, out_ref, start, stop, base):
    q_at, k_at, own = slice(start, stop), slice(0, stop), slice(start - base, stop - base)
    for head in range(expo_ref.shape[0]):
        at = lanes(head)
        scores = dot_nt(qkv_ref[0, q_at, at], qkv_ref[1, k_at, at])
        rows = lax.broadcasted_iota(jnp.int32, scores.shape, 0) + start
        cols = lax.broadcasted_iota(jnp.int32, scores.shape, 1)
        scores = jnp.where(cols <= rows, scores, -jnp.inf)
        peak = jnp.max(scores, axis=1, keepdims=True)
        expo = jnp.exp2((scores - peak) * FACTOR).astype(jnp.bfloat16)
        expo_ref[head, own, k_at] = expo
        both = dot_nn(expo, values_ref[k_at, lanes(head, 2)])
        inverse = 1.0 / both[:, HD:]
        inverse_ref[own, at] = inverse
        out_ref[q_at, at] = (both[:, :HD] * inverse).astype(jnp.bfloat16)


def set_values(qkv_ref, values_ref, start, stop):
    for head in range(qkv_ref.shape[2] // HD):
        values_ref[start:stop, 2 * head * HD : (2 * head + 1) * HD] = qkv_ref[2, start:stop, lanes(head)]
        values_ref[start:stop, (2 * head + 1) * HD : (2 * head + 2) * HD] = jnp.ones((stop - start, HD), jnp.bfloat16)


def first_kernel(
    half,
    qkv_hbm,
    dout_hbm,
    out_ref,
    relay_ref,
    expo_ref,
    inverse_ref,
    qkv_ref,
    dout_ref,
    values_ref,
    qkv_sem,
    dout_sem,
):
    cut = relay_ref.shape[0]
    length = qkv_ref.shape[1]
    chunks = []
    for k, (start, stop) in enumerate(((0, BLK), (BLK, cut), (cut, length))):
        chunks.append(pltpu.make_async_copy(qkv_hbm.at[:, start:stop], qkv_ref.at[:, start:stop], qkv_sem.at[k]))
    fetch = pltpu.make_async_copy(dout_hbm, dout_ref, dout_sem)
    chunks[0].start()
    chunks[1].start()
    fetch.start()
    chunks[2].start()
    for k, (start, stop) in enumerate(((0, BLK), (BLK, cut))):
        chunks[k].wait()
        set_values(qkv_ref, values_ref, start, stop)
        attend(qkv_ref, values_ref, expo_ref, inverse_ref, out_ref, start, stop, 0)
    rest = expo_ref.shape[2] - cut
    expo_ref[:, BLK:cut, cut:] = jnp.zeros((expo_ref.shape[0], cut - BLK, rest), jnp.bfloat16)
    fetch.wait()
    sends_dout = lax.rem(lax.axis_index(SECTION), half) == 0

    @pl.when(sends_dout)
    def _():
        relay_ref[...] = dout_ref[0:cut]

    @pl.when(jnp.logical_not(sends_dout))
    def _():
        relay_ref[...] = out_ref[...]

    chunks[2].wait()


def second_kernel(half, qkv_ref, dout_ref, early_ref, out_ref, direct_ref, expo_ref, inverse_ref, values_ref):
    length, width = out_ref.shape
    cut = early_ref.shape[0]
    set_values(qkv_ref, values_ref, 0, length)
    out_ref[0:cut] = early_ref[...]
    for start, stop in ((cut, 2 * BLK), (2 * BLK, length)):
        attend(qkv_ref, values_ref, expo_ref, inverse_ref, out_ref, start, stop, cut)
    sends_dout = lax.rem(lax.axis_index(SECTION), half) == 0

    @pl.when(sends_dout)
    def _():
        direct_ref[...] = dout_ref[cut:length]

    @pl.when(jnp.logical_not(sends_dout))
    def _():
        direct_ref[...] = out_ref[cut:length]


def gradients(refs, parts, grads_ref, dout_ref, stage_ref, grads_sem):
    qkv_ref, early_ref, late_ref, values_ref, out_ref = refs
    length, width = out_ref.shape
    heads = width // HD
    cut = early_ref.shape[1]
    n = length // BLK
    copies = []

    def expo_of(head, i, cols):
        start, stop = i * BLK, (i + 1) * BLK
        pieces = []
        if start < cut:
            pieces.append(early_ref[head, start : min(stop, cut), cols])
        if stop > cut:
            pieces.append(late_ref[head, max(start, cut) - cut : stop - cut, cols])
        return pieces[0] if len(pieces) == 1 else jnp.concatenate(pieces, axis=0)

    for head in range(heads):
        at, wide = lanes(head), lanes(head, 2)
        left = slice(2 * head * HD, (2 * head + 1) * HD)
        right = slice((2 * head + 1) * HD, (2 * head + 2) * HD)
        for start, stop, inverse_ref, ref in parts:
            scaled = ref[:, at].astype(jnp.float32) * inverse_ref[:, at]
            dout_ref[start:stop, left] = scaled.astype(jnp.bfloat16)
            product = scaled * out_ref[start:stop, at].astype(jnp.float32)
            dout_ref[start:stop, right] = (-product).astype(jnp.bfloat16)
        dk, dv = [None] * n, [None] * n
        for i in range(n):
            q_at, k_at = slice(i * BLK, (i + 1) * BLK), slice(0, (i + 1) * BLK)
            expo = expo_of(head, i, k_at)
            grad_p = dot_nt(dout_ref[q_at, wide], values_ref[k_at, wide])
            grad_s = (expo.astype(jnp.float32) * grad_p).astype(jnp.bfloat16)
            stage_ref[0, q_at, at] = (dot_nn(grad_s, qkv_ref[1, k_at, at]) * SCALE).astype(jnp.bfloat16)
            for j in range(i + 1):
                sub = slice(j * BLK, (j + 1) * BLK)
                kk = dot_tn(grad_s[:, sub], qkv_ref[0, q_at, at])
                vv = dot_tn(expo[:, sub], dout_ref[q_at, left])
                dk[j] = kk if dk[j] is None else dk[j] + kk
                dv[j] = vv if dv[j] is None else dv[j] + vv
        for j in range(n):
            sub = slice(j * BLK, (j + 1) * BLK)
            stage_ref[1, sub, at] = (dk[j] * SCALE).astype(jnp.bfloat16)
            stage_ref[2, sub, at] = dv[j].astype(jnp.bfloat16)
        copy = pltpu.make_async_copy(stage_ref.at[:, :, at], grads_ref.at[:, :, at], grads_sem.at[head])
        copy.start()
        copies.append(copy)
    for copy in copies:
        copy.wait()


def near_kernel(half, *refs):
    held, (first_ref, second_ref), (near_ref, _, grads_ref, passed_ref), work = refs[:5], refs[5:7], refs[7:11], refs[11:]
    cut, length = first_ref.shape[0], near_ref.shape[0]
    passed_ref[...] = held[4][...]

    @pl.when(lax.rem(lax.axis_index(SECTION), half) != half - 1)
    def _():
        parts = [(0, cut, first_ref, near_ref.at[0:cut]), (cut, length, second_ref, near_ref.at[cut:length])]
        gradients(held, parts, grads_ref, *work)


def far_kernel(half, _, *refs):
    held, (first_ref, second_ref, relay_ref, direct_ref, grads_ref, token_ref), work = refs[:5], refs[5:11], refs[11:]
    token_ref[...] = jnp.zeros_like(token_ref)
    cut, length = first_ref.shape[0], held[4].shape[0]

    @pl.when(lax.rem(lax.axis_index(SECTION), half) == half - 1)
    def _():
        parts = [(0, cut, first_ref, relay_ref), (cut, length, second_ref, direct_ref)]
        gradients(held, parts, grads_ref, *work)


def emit_kernel(half, _, near_ref, relay_ref, direct_ref, attn_ref, sem):
    cut, length = relay_ref.shape[0], attn_ref.shape[0]
    place = lax.rem(lax.axis_index(SECTION), half)
    parts = [(0, cut, relay_ref), (cut, length, direct_ref)]

    def send(k, source):
        return pltpu.make_async_copy(source, attn_ref.at[parts[k][0] : parts[k][1]], sem.at[k])

    @pl.when(place == 0)
    def _():
        for k, part in enumerate(parts):
            send(k, part[2]).start()

    @pl.when(place != 0)
    def _():
        for k, part in enumerate(parts):
            send(k, near_ref.at[part[0] : part[1]]).start()

    for k, part in enumerate(parts):
        send(k, near_ref.at[part[0] : part[1]]).wait()


VMEM = pl.BlockSpec(memory_space=pltpu.VMEM)
HBM = pl.BlockSpec(memory_space=pltpu.HBM)
ANY = pl.BlockSpec(memory_space=pl.ANY)
FIRST_LIMIT = 48 * 2**20


def on_device(qkv_sent, grad_out):
    bf16 = jnp.bfloat16
    qkv = qkv_sent[0].transpose(1, 0, 2)
    dout = grad_out[0]
    _, length, width = qkv.shape
    heads = width // HD
    cut = length // 2
    count = lax.axis_size(SECTION)
    half = count // 2
    last = half - 1
    work = heads * length * length * HD
    whole = jax.ShapeDtypeStruct((length, width), bf16)
    part = jax.ShapeDtypeStruct((cut, width), bf16)
    three = jax.ShapeDtypeStruct(qkv.shape, bf16)
    inverse = jax.ShapeDtypeStruct((cut, width), jnp.float32)
    params = pltpu.CompilerParams(vmem_limit_bytes=24 * 2**20)
    scratch = [
        pltpu.VMEM((length, 2 * width), bf16),
        pltpu.VMEM(qkv.shape, bf16),
        pltpu.SemaphoreType.DMA((heads,)),
    ]

    def cost(flops):
        return pl.CostEstimate(flops=flops, bytes_accessed=12 * length * width, transcendentals=0)

    early_out, relay, early, inverse0, held, held_dout = pl.pallas_call(
        lambda *refs: first_kernel(half, *refs),
        out_shape=(part, part, jax.ShapeDtypeStruct((heads, cut, 2 * BLK), bf16), inverse, three, whole),
        in_specs=[HBM] * 2,
        out_specs=(VMEM,) * 6,
        scratch_shapes=[
            pltpu.VMEM((cut, 2 * width), bf16),
            pltpu.SemaphoreType.DMA((3,)),
            pltpu.SemaphoreType.DMA,
        ],
        name="first",
        compiler_params=pltpu.CompilerParams(vmem_limit_bytes=FIRST_LIMIT),
        cost_estimate=cost(work),
    )(qkv, dout)
    relay = lax.ppermute(relay, SECTION, same_pairs(count, half, [(0, 2), (last, last - 2)]))
    near_dout = lax.ppermute(held_dout, SECTION, near_pairs(count, half, -1))
    out, direct, late, inverse1, values = pl.pallas_call(
        lambda *refs: second_kernel(half, *refs),
        out_shape=(
            whole,
            part,
            jax.ShapeDtypeStruct((heads, length - cut, length), bf16),
            inverse,
            jax.ShapeDtypeStruct((length, 2 * width), bf16),
        ),
        in_specs=[VMEM] * 3,
        out_specs=(VMEM,) * 5,
        name="second",
        compiler_params=params,
        cost_estimate=cost(40 * work),
    )(held, held_dout, early_out)
    relay_hop = relay
    relay, direct = lax.optimization_barrier((relay, direct))
    relay = lax.ppermute(relay, SECTION, far_pairs(count, half, [(2, last), (last - 2, 0)]))
    direct = lax.ppermute(direct, SECTION, far_pairs(count, half, [(0, last), (last, 0)]))
    kept = (held, early, late, values, out, inverse0, inverse1)
    grads, passed = pl.pallas_call(
        lambda *refs: near_kernel(half, *refs),
        out_shape=(three, whole),
        in_specs=[VMEM] * 8 + [ANY],
        out_specs=(HBM, VMEM),
        scratch_shapes=scratch,
        name="near",
        compiler_params=params,
        cost_estimate=cost(4 * work),
    )(*kept, near_dout, relay_hop)
    near_out = lax.ppermute(passed, SECTION, near_pairs(count, half, 1))
    grads, token = pl.pallas_call(
        lambda *refs: far_kernel(half, *refs),
        out_shape=(three, jax.ShapeDtypeStruct((8, HD), jnp.float32)),
        in_specs=[HBM] + [VMEM] * 9,
        out_specs=(HBM, VMEM),
        scratch_shapes=scratch,
        input_output_aliases={0: 0},
        name="far",
        compiler_params=params,
        cost_estimate=cost(40 * work),
    )(grads, *kept, relay, direct)
    attn_out = pl.pallas_call(
        lambda *refs: emit_kernel(half, *refs),
        out_shape=whole,
        in_specs=[ANY] * 4,
        out_specs=HBM,
        scratch_shapes=[pltpu.SemaphoreType.DMA((2,))],
        name="emit",
        compiler_params=pltpu.CompilerParams(vmem_limit_bytes=2**20),
        cost_estimate=cost(1),
    )(token, near_out, relay, direct)
    return (attn_out[None], grads.transpose(1, 0, 2)[None])


def solution(mesh):
    in_specs = (P("section", None, None, "tp"), P("section", None, "tp"))
    out_specs = (P("section", None, "tp"), P("section", None, None, "tp"))
    return jax.shard_map(
        on_device, mesh=mesh, in_specs=in_specs, out_specs=out_specs, check_vma=False
    )
```

time: 50.4 us -> 47.2 us (0.937)
  the two profiles are of different devices: /device:TPU:38 before, /device:TPU:63 now
where the time goes in v3:
time: 47.2 us; the launch traced here: 46.9 us
  starting transfers between devices  21.5 us (46%)
  waiting for transfers between devices  14.7 us (31%)
  Pallas kernels  8.88 us (19%)
  local copies, waits for them, and re-layouts  1.06 us (2%)
  between operations  0.73 us (2%)
    ppermute x1, starting transfers between devices, on_device(): lax.ppermute(direct, SECTION, far_pairs(count, half, [(0, last), (last, 0...  15.2 us
    ppermute x1, waiting for transfers between devices, on_device(): lax.ppermute(relay, SECTION, far_pairs(count, half, [(2, last), (last - 2...  12.6 us
    pallas_call x1, Pallas kernels, on_device(): pl.pallas_call(lambda *refs: far_kernel(half, *refs), out_shape=(three, j...  4.14 us
    ppermute x1, starting transfers between devices, on_device(): lax.ppermute(relay, SECTION, same_pairs(count, half, [(0, 2), (last, last...  2.39 us
    pallas_call x1, Pallas kernels, on_device(): pl.pallas_call(lambda *refs: first_kernel(half, *refs), out_shape=(part,...  2.31 us
    ppermute x1, waiting for transfers between devices, on_device(): lax.ppermute(relay, SECTION, same_pairs(count, half, [(0, 2), (last, last...  2 us
    pallas_call x1, Pallas kernels, on_device(): pl.pallas_call(lambda *refs: second_kernel(half, *refs), out_shape=(whole...  1.51 us
    ppermute x1, starting transfers between devices, on_device(): near_dout = lax.ppermute(held_dout, SECTION, near_pairs(count, half, -1))  1.33 us
  transfers between devices with their start and end apart: 5, of which 3 were waited for; matrix products, arithmetic and copies ran while one was open for 0% of the time, Pallas kernels for 12%

profile of v3, /device:TPU:63, one launch (start us, length us, event | category | flops | bytes accessed | tf_op | source)
XLA Modules:
  0.0 46.9 jit_solution(3353947737888089297)
XLA Ops:
  0.6 0.0 copy-start
  0.6 1.1 %copy-done = bf16[1,768,384]{2,1,0:T(8,128)(2,1)S(1)} copy-done((bf16[1,768,384]{2,1,0:T(8,128)(2,1)S(1)}, bf16[1,768,384]{2,1,0:T(8,128)(2,1)}, u32[]{:S(2)}) %copy-start) | copy-done | bytes 589848
  1.7 2.3 %first.1 = (bf16[384,384]{1,0:T(8,128)(2,1)S(1)}, bf16[384,384]{1,0:T(8,128)(2,1)S(1)}, bf16[3,384,512]{2,1,0:T(8,128)(2,1)S(1)}, f32[384,384]{1,0:T(8,128)S(1)}...) custom-call(bf16[3,768,384]{2,1,0:T(8,128)(2,1)} %bitcast.9, bf16[768,384]{1,0:T(8,128)(2,1)S(1)} %bitcast.8), custom_call_target="tpu_custom_call" | custom-call | flops 226492416 | bytes 3538944 | tf_op jit(solution)/shard_map/first/pallas_call | solution.py:259
  4.0 2.4 %collective-permute-start.1 = (bf16[384,384]{1,0:T(8,128)(2,1)S(1)}, bf16[384,384]{1,0:T(8,128)(2,1)S(1)}, u32[]{:S(2)}, u32[]{:S(2)}) collective-permute-start(bf16[384,384]{1,0:T(8,128)(2,1)S(1)} %get-tuple-element.28), channel_id=1, source_target_pairs={{0,64},{224,160},{256,320},{480,416},{1,65},{225,161},{257,321},{4... | collective-permute-start | bytes 884744 | tf_op jit(solution)/shard_map/ppermute | solution.py:273
  6.4 1.3 %collective-permute-start = (bf16[768,384]{1,0:T(8,128)(2,1)S(1)}, bf16[768,384]{1,0:T(8,128)(2,1)S(1)}, u32[]{:S(2)}, u32[]{:S(2)}) collective-permute-start(bf16[768,384]{1,0:T(8,128)(2,1)S(1)} %get-tuple-element.21.refs_1_), channel_id=1, source_target_pairs={{32,0},{64,32},{96,64},{128,96},{160,128},{192,160},{224,192},{288... | collective-permute-start | bytes 1769480 | tf_op jit(solution)/shard_map/ppermute | solution.py:274
  7.7 1.5 %second.1 = (bf16[768,384]{1,0:T(8,128)(2,1)S(1)}, bf16[384,384]{1,0:T(8,128)(2,1)S(1)}, bf16[3,384,768]{2,1,0:T(8,128)(2,1)S(1)}, f32[384,384]{1,0:T(8,128)S(1)}, bf16[768,768]{1,0:T(8,128)(2,1)S(1)}) custom-call(bf16[3,768,384]{2,1,0:T(8,128)(2,1)S(1)} %get-tuple-element.19.refs_0_.refs_1_, bf16[768,384]{1,0:T(8,128)(2,1)S(1)} %get-tuple-element.21.refs_1_, ...), custom_call_target="tpu_custom_call" | custom-call | flops 9059696640 | bytes 3538944 | tf_op jit(solution)/shard_map/second/pallas_call | solution.py:275
  9.3 2.0 %collective-permute-done.1.refs_8_ = bf16[384,384]{1,0:T(8,128)(2,1)S(1)} collective-permute-done((bf16[384,384]{1,0:T(8,128)(2,1)S(1)}, bf16[384,384]{1,0:T(8,128)(2,1)S(1)}, u32[]{:S(2)}, u32[]{:S(2)}) %collective-permute-start.1) | collective-permute-done | bytes 294944 | tf_op jit(solution)/shard_map/ppermute | solution.py:273
  11.3 1.3 %collective-permute-start.2 = (bf16[384,384]{1,0:T(8,128)(2,1)S(1)}, bf16[384,384]{1,0:T(8,128)(2,1)S(1)}, u32[]{:S(2)}, u32[]{:S(2)}) collective-permute-start(bf16[384,384]{1,0:T(8,128)(2,1)S(1)} %collective-permute-done.1.refs_8_), channel_id=1, source_target_pairs={{64,480},{160,256},{320,224},{416,0},{65,481},{161,257},{321,225},... | collective-permute-start | bytes 884744 | tf_op jit(solution)/shard_map/ppermute | solution.py:292
  12.5 15.2 %collective-permute-start.3 = (bf16[384,384]{1,0:T(8,128)(2,1)S(1)}, bf16[384,384]{1,0:T(8,128)(2,1)S(1)}, u32[]{:S(2)}, u32[]{:S(2)}) collective-permute-start(bf16[384,384]{1,0:T(8,128)(2,1)S(1)} %get-tuple-element.32), channel_id=1, source_target_pairs={{0,480},{224,256},{256,224},{480,0},{1,481},{225,257},{257,225},{4... | collective-permute-start | bytes 884744 | tf_op jit(solution)/shard_map/ppermute | solution.py:293
  27.8 0.0 collective-permute-done.refs_7_
  27.8 0.1 near.1
  27.9 1.3 %collective-permute-start.4 = (bf16[768,384]{1,0:T(8,128)(2,1)S(1)}, bf16[768,384]{1,0:T(8,128)(2,1)S(1)}, u32[]{:S(2)}, u32[]{:S(2)}) collective-permute-start(bf16[768,384]{1,0:T(8,128)(2,1)S(1)} %get-tuple-element.34), channel_id=1, source_target_pairs={{0,32},{32,64},{64,96},{96,128},{128,160},{160,192},{192,224},{256... | collective-permute-start | bytes 1769480 | tf_op jit(solution)/shard_map/ppermute | solution.py:305
  29.2 12.6 %collective-permute-done.2.refs_8_.refs_2_ = bf16[384,384]{1,0:T(8,128)(2,1)S(1)} collective-permute-done((bf16[384,384]{1,0:T(8,128)(2,1)S(1)}, bf16[384,384]{1,0:T(8,128)(2,1)S(1)}, u32[]{:S(2)}, u32[]{:S(2)}) %collective-permute-start.2) | collective-permute-done | bytes 294944 | tf_op jit(solution)/shard_map/ppermute | solution.py:292
  41.8 0.1 collective-permute-done.3.refs_9_.refs_3_
  41.9 4.1 %far.1 = (bf16[3,768,384]{2,1,0:T(8,128)(2,1)}, f32[8,128]{1,0:T(8,128)S(1)}) custom-call(bf16[3,768,384]{2,1,0:T(8,128)(2,1)} %get-tuple-element.29.refs_0_, bf16[3,768,384]{2,1,0:T(8,128)(2,1)S(1)} %get-tuple-element.19.refs_0_.refs_1_, bf16[3,384,512]{2,1,0:T(8,128)(2,1)S(1)} %get-tuple-element.20.refs_1_.refs_2_, ...), custom_call_target="tpu_custom_call", output_to_operand_aliasing={{0}: (0, {})} | custom-call | flops 9059696640 | bytes 3538944 | tf_op jit(solution)/shard_map/far/pallas_call | solution.py:306
  46.0 0.0 collective-permute-done.4.refs_1_
  46.1 0.8 %emit.1 = bf16[768,384]{1,0:T(8,128)(2,1)} custom-call(f32[8,128]{1,0:T(8,128)S(1)} %get-tuple-element.33.refs_0_, bf16[768,384]{1,0:T(8,128)(2,1)S(1)} %collective-permute-done.4.refs_1_, bf16[384,384]{1,0:T(8,128)(2,1)S(1)} %collective-permute-done.2.refs_8_.refs_2_, bf16[384,384]{1,0:T(8,128)(2,1)S(1)} %collective-permute-done.3.refs_9_.refs_3_), custom_call_target="tpu_custom_call" | custom-call | flops 1 | bytes 3538944 | tf_op jit(solution)/shard_map/emit/pallas_call | solution.py:317
Async XLA Ops:
  0.6 1.1 %copy-start = (bf16[1,768,384]{2,1,0:T(8,128)(2,1)S(1)}, bf16[1,768,384]{2,1,0:T(8,128)(2,1)}, u32[]{:S(2)}) copy-start(bf16[1,768,384]{2,1,0:T(8,128)(2,1)} %param.3) | copy-start | bytes 1769476
  4.0 7.2 %collective-permute-start.1 = (bf16[384,384]{1,0:T(8,128)(2,1)S(1)}, bf16[384,384]{1,0:T(8,128)(2,1)S(1)}, u32[]{:S(2)}, u32[]{:S(2)}) collective-permute-start(bf16[384,384]{1,0:T(8,128)(2,1)S(1)} %get-tuple-element.28), channel_id=1, source_target_pairs={{0,64},{224,160},{256,320},{480,416},{1,65},{225,161},{257,321},{4... | collective-permute-start | bytes 884744 | tf_op jit(solution)/shard_map/ppermute | solution.py:273
  6.4 21.4 %collective-permute-start = (bf16[768,384]{1,0:T(8,128)(2,1)S(1)}, bf16[768,384]{1,0:T(8,128)(2,1)S(1)}, u32[]{:S(2)}, u32[]{:S(2)}) collective-permute-start(bf16[768,384]{1,0:T(8,128)(2,1)S(1)} %get-tuple-element.21.refs_1_), channel_id=1, source_target_pairs={{32,0},{64,32},{96,64},{128,96},{160,128},{192,160},{224,192},{288... | collective-permute-start | bytes 1769480 | tf_op jit(solution)/shard_map/ppermute | solution.py:274
  11.3 30.6 %collective-permute-start.2 = (bf16[384,384]{1,0:T(8,128)(2,1)S(1)}, bf16[384,384]{1,0:T(8,128)(2,1)S(1)}, u32[]{:S(2)}, u32[]{:S(2)}) collective-permute-start(bf16[384,384]{1,0:T(8,128)(2,1)S(1)} %collective-permute-done.1.refs_8_), channel_id=1, source_target_pairs={{64,480},{160,256},{320,224},{416,0},{65,481},{161,257},{321,225},... | collective-permute-start | bytes 884744 | tf_op jit(solution)/shard_map/ppermute | solution.py:292
  12.5 29.4 %collective-permute-start.3 = (bf16[384,384]{1,0:T(8,128)(2,1)S(1)}, bf16[384,384]{1,0:T(8,128)(2,1)S(1)}, u32[]{:S(2)}, u32[]{:S(2)}) collective-permute-start(bf16[384,384]{1,0:T(8,128)(2,1)S(1)} %get-tuple-element.32), channel_id=1, source_target_pairs={{0,480},{224,256},{256,224},{480,0},{1,481},{225,257},{257,225},{4... | collective-permute-start | bytes 884744 | tf_op jit(solution)/shard_map/ppermute | solution.py:293
  27.9 18.2 %collective-permute-start.4 = (bf16[768,384]{1,0:T(8,128)(2,1)S(1)}, bf16[768,384]{1,0:T(8,128)(2,1)S(1)}, u32[]{:S(2)}, u32[]{:S(2)}) collective-permute-start(bf16[768,384]{1,0:T(8,128)(2,1)S(1)} %get-tuple-element.34), channel_id=1, source_target_pairs={{0,32},{32,64},{64,96},{96,128},{128,160},{160,192},{192,224},{256... | collective-permute-start | bytes 1769480 | tf_op jit(solution)/shard_map/ppermute | solution.py:305

commit v4 on v3

--- a/solution.py
+++ b/solution.py
@@ -69,48 +69,33 @@
         values_ref[start:stop, (2 * head + 1) * HD : (2 * head + 2) * HD] = jnp.ones((stop - start, HD), jnp.bfloat16)
 
 
-def first_kernel(
-    half,
-    qkv_hbm,
-    dout_hbm,
-    out_ref,
-    relay_ref,
-    expo_ref,
-    inverse_ref,
-    qkv_ref,
-    dout_ref,
-    values_ref,
-    qkv_sem,
-    dout_sem,
-):
-    cut = relay_ref.shape[0]
+def first_kernel(qkv_hbm, out_ref, expo_ref, inverse_ref, qkv_ref, values_ref, qkv_sem):
+    cut = out_ref.shape[0]
     length = qkv_ref.shape[1]
     chunks = []
     for k, (start, stop) in enumerate(((0, BLK), (BLK, cut), (cut, length))):
         chunks.append(pltpu.make_async_copy(qkv_hbm.at[:, start:stop], qkv_ref.at[:, start:stop], qkv_sem.at[k]))
-    fetch = pltpu.make_async_copy(dout_hbm, dout_ref, dout_sem)
-    chunks[0].start()
-    chunks[1].start()
-    fetch.start()
-    chunks[2].start()
+        chunks[k].start()
     for k, (start, stop) in enumerate(((0, BLK), (BLK, cut))):
         chunks[k].wait()
         set_values(qkv_ref, values_ref, start, stop)
         attend(qkv_ref, values_ref, expo_ref, inverse_ref, out_ref, start, stop, 0)
     rest = expo_ref.shape[2] - cut
     expo_ref[:, BLK:cut, cut:] = jnp.zeros((expo_ref.shape[0], cut - BLK, rest), jnp.bfloat16)
-    fetch.wait()
+    chunks[2].wait()
+
+
+def pick_kernel(half, out_ref, dout_ref, relay_ref, held_ref):
     sends_dout = lax.rem(lax.axis_index(SECTION), half) == 0
+    held_ref[...] = dout_ref[...]
 
     @pl.when(sends_dout)
     def _():
-        relay_ref[...] = dout_ref[0:cut]
+        relay_ref[...] = dout_ref[0 : relay_ref.shape[0]]
 
     @pl.when(jnp.logical_not(sends_dout))
     def _():
         relay_ref[...] = out_ref[...]
-
-    chunks[2].wait()
 
 
 def second_kernel(half, qkv_ref, dout_ref, early_ref, out_ref, direct_ref, expo_ref, inverse_ref, values_ref):
@@ -131,16 +116,14 @@
         direct_ref[...] = out_ref[cut:length]
 
 
-def gradients(refs, parts, grads_ref, dout_ref, stage_ref, grads_sem):
+def gradients(refs, parts, grads_ref, dout_ref, stage_ref, scores_ref, sums_ref, grads_sem):
     qkv_ref, early_ref, late_ref, values_ref, out_ref = refs
     length, width = out_ref.shape
     heads = width // HD
     cut = early_ref.shape[1]
-    n = length // BLK
     copies = []
 
-    def expo_of(head, i, cols):
-        start, stop = i * BLK, (i + 1) * BLK
+    def expo_of(head, start, stop, cols):
         pieces = []
         if start < cut:
             pieces.append(early_ref[head, start : min(stop, cut), cols])
@@ -157,23 +140,24 @@
             dout_ref[start:stop, left] = scaled.astype(jnp.bfloat16)
             product = scaled * out_ref[start:stop, at].astype(jnp.float32)
             dout_ref[start:stop, right] = (-product).astype(jnp.bfloat16)
-        dk, dv = [None] * n, [None] * n
-        for i in range(n):
-            q_at, k_at = slice(i * BLK, (i + 1) * BLK), slice(0, (i + 1) * BLK)
-            expo = expo_of(head, i, k_at)
+        for first in range(0, length, BLK):
+            k_at, q_at = slice(first, first + BLK), slice(first, length)
             grad_p = dot_nt(dout_ref[q_at, wide], values_ref[k_at, wide])
+            expo = expo_of(head, first, length, k_at)
             grad_s = (expo.astype(jnp.float32) * grad_p).astype(jnp.bfloat16)
-            stage_ref[0, q_at, at] = (dot_nn(grad_s, qkv_ref[1, k_at, at]) * SCALE).astype(jnp.bfloat16)
-            for j in range(i + 1):
-                sub = slice(j * BLK, (j + 1) * BLK)
-                kk = dot_tn(grad_s[:, sub], qkv_ref[0, q_at, at])
-                vv = dot_tn(expo[:, sub], dout_ref[q_at, left])
-                dk[j] = kk if dk[j] is None else dk[j] + kk
-                dv[j] = vv if dv[j] is None else dv[j] + vv
-        for j in range(n):
-            sub = slice(j * BLK, (j + 1) * BLK)
-            stage_ref[1, sub, at] = (dk[j] * SCALE).astype(jnp.bfloat16)
-            stage_ref[2, sub, at] = dv[j].astype(jnp.bfloat16)
+            scores_ref[q_at, k_at] = grad_s
+            dq = dot_nn(grad_s, qkv_ref[1, k_at, at])
+            sums_ref[0, q_at] = dq if first == 0 else sums_ref[0, q_at] + dq
+        stage_ref[0, :, at] = (sums_ref[0] * SCALE).astype(jnp.bfloat16)
+        for first in reversed(range(0, length, BLK)):
+            q_at, k_at = slice(first, first + BLK), slice(0, first + BLK)
+            dk = dot_tn(scores_ref[q_at, k_at], qkv_ref[0, q_at, at])
+            dv = dot_tn(expo_of(head, first, first + BLK, k_at), dout_ref[q_at, left])
+            last = first + BLK == length
+            sums_ref[1, k_at] = dk if last else sums_ref[1, k_at] + dk
+            sums_ref[2, k_at] = dv if last else sums_ref[2, k_at] + dv
+        stage_ref[1, :, at] = (sums_ref[1] * SCALE).astype(jnp.bfloat16)
+        stage_ref[2, :, at] = sums_ref[2].astype(jnp.bfloat16)
         copy = pltpu.make_async_copy(stage_ref.at[:, :, at], grads_ref.at[:, :, at], grads_sem.at[head])
         copy.start()
         copies.append(copy)
@@ -228,7 +212,7 @@
 VMEM = pl.BlockSpec(memory_space=pltpu.VMEM)
 HBM = pl.BlockSpec(memory_space=pltpu.HBM)
 ANY = pl.BlockSpec(memory_space=pl.ANY)
-FIRST_LIMIT = 48 * 2**20
+FIRST_LIMIT = 49 * 2**20
 
 
 def on_device(qkv_sent, grad_out):
@@ -250,26 +234,33 @@
     scratch = [
         pltpu.VMEM((length, 2 * width), bf16),
         pltpu.VMEM(qkv.shape, bf16),
+        pltpu.VMEM((length, length), bf16),
+        pltpu.VMEM((3, length, HD), jnp.float32),
         pltpu.SemaphoreType.DMA((heads,)),
     ]
 
     def cost(flops):
         return pl.CostEstimate(flops=flops, bytes_accessed=12 * length * width, transcendentals=0)
 
-    early_out, relay, early, inverse0, held, held_dout = pl.pallas_call(
-        lambda *refs: first_kernel(half, *refs),
-        out_shape=(part, part, jax.ShapeDtypeStruct((heads, cut, 2 * BLK), bf16), inverse, three, whole),
-        in_specs=[HBM] * 2,
-        out_specs=(VMEM,) * 6,
-        scratch_shapes=[
-            pltpu.VMEM((cut, 2 * width), bf16),
-            pltpu.SemaphoreType.DMA((3,)),
-            pltpu.SemaphoreType.DMA,
-        ],
+    early_out, early, inverse0, held = pl.pallas_call(
+        first_kernel,
+        out_shape=(part, jax.ShapeDtypeStruct((heads, cut, 2 * BLK), bf16), inverse, three),
+        in_specs=[HBM],
+        out_specs=(VMEM,) * 4,
+        scratch_shapes=[pltpu.VMEM((cut, 2 * width), bf16), pltpu.SemaphoreType.DMA((3,))],
         name="first",
         compiler_params=pltpu.CompilerParams(vmem_limit_bytes=FIRST_LIMIT),
         cost_estimate=cost(work),
-    )(qkv, dout)
+    )(qkv)
+    relay, held_dout = pl.pallas_call(
+        lambda *refs: pick_kernel(half, *refs),
+        out_shape=(part, whole),
+        in_specs=[VMEM] * 2,
+        out_specs=(VMEM,) * 2,
+        name="pick",
+        compiler_params=pltpu.CompilerParams(vmem_limit_bytes=4 * 2**20),
+        cost_estimate=cost(1),
+    )(early_out, dout)
     relay = lax.ppermute(relay, SECTION, same_pairs(count, half, [(0, 2), (last, last - 2)]))
     near_dout = lax.ppermute(held_dout, SECTION, near_pairs(count, half, -1))
     out, direct, late, inverse1, values = pl.pallas_call(

time: 47.2 us -> 45.8 us (0.970)
  the two profiles are of different devices: /device:TPU:63 before, /device:TPU:61 now
where the time goes in v4:
time: 45.8 us; the launch traced here: 45.6 us
  starting transfers between devices  21.5 us (47%)
  waiting for transfers between devices  14.7 us (32%)
  Pallas kernels  8.65 us (19%)
  between operations  0.74 us (2%)
    ppermute x1, starting transfers between devices, on_device(): lax.ppermute(direct, SECTION, far_pairs(count, half, [(0, last), (last, 0...  15.2 us
    ppermute x1, waiting for transfers between devices, on_device(): lax.ppermute(relay, SECTION, far_pairs(count, half, [(2, last), (last - 2...  12.7 us
    pallas_call x1, Pallas kernels, on_device(): pl.pallas_call(lambda *refs: far_kernel(half, *refs), out_shape=(three, j...  3.81 us
    ppermute x1, starting transfers between devices, on_device(): lax.ppermute(relay, SECTION, same_pairs(count, half, [(0, 2), (last, last...  2.39 us
    pallas_call x1, Pallas kernels, on_device(): pl.pallas_call(first_kernel, out_shape=(part, jax.ShapeDtypeStruct((heads...  2.32 us
    ppermute x1, waiting for transfers between devices, on_device(): lax.ppermute(relay, SECTION, same_pairs(count, half, [(0, 2), (last, last...  2 us
    pallas_call x1, Pallas kernels, on_device(): pl.pallas_call(lambda *refs: second_kernel(half, *refs), out_shape=(whole...  1.51 us
    ppermute x1, starting transfers between devices, on_device(): near_dout = lax.ppermute(held_dout, SECTION, near_pairs(count, half, -1))  1.33 us
  transfers between devices with their start and end apart: 5, of which 2 were waited for; matrix products, arithmetic and copies ran while one was open for 0% of the time, Pallas kernels for 12%

profile of v4, /device:TPU:61, one launch (start us, length us, event | category | flops | bytes accessed | tf_op | source)
XLA Modules:
  0.0 45.6 jit_solution(1716394038435507259)
XLA Ops:
  0.6 0.0 copy-start
  0.6 2.3 %first.1 = (bf16[384,384]{1,0:T(8,128)(2,1)S(1)}, bf16[3,384,512]{2,1,0:T(8,128)(2,1)S(1)}, f32[384,384]{1,0:T(8,128)S(1)}, bf16[3,768,384]{2,1,0:T(8,128)(2,1)S(1)}) custom-call(bf16[3,768,384]{2,1,0:T(8,128)(2,1)} %bitcast.9), custom_call_target="tpu_custom_call" | custom-call | flops 226492416 | bytes 3538944 | tf_op jit(solution)/shard_map/first/pallas_call | solution.py:245
  3.0 0.0 copy-done
  3.0 0.1 pick.1
  3.1 2.4 %collective-permute-start.1 = (bf16[384,384]{1,0:T(8,128)(2,1)S(1)}, bf16[384,384]{1,0:T(8,128)(2,1)S(1)}, u32[]{:S(2)}, u32[]{:S(2)}) collective-permute-start(bf16[384,384]{1,0:T(8,128)(2,1)S(1)} %get-tuple-element.28), channel_id=1, source_target_pairs={{0,64},{224,160},{256,320},{480,416},{1,65},{225,161},{257,321},{4... | collective-permute-start | bytes 884744 | tf_op jit(solution)/shard_map/ppermute | solution.py:264
  5.5 1.3 %collective-permute-start = (bf16[768,384]{1,0:T(8,128)(2,1)S(1)}, bf16[768,384]{1,0:T(8,128)(2,1)S(1)}, u32[]{:S(2)}, u32[]{:S(2)}) collective-permute-start(bf16[768,384]{1,0:T(8,128)(2,1)S(1)} %get-tuple-element.22.refs_1_), channel_id=1, source_target_pairs={{32,0},{64,32},{96,64},{128,96},{160,128},{192,160},{224,192},{288... | collective-permute-start | bytes 1769480 | tf_op jit(solution)/shard_map/ppermute | solution.py:265
  6.8 1.5 %second.1 = (bf16[768,384]{1,0:T(8,128)(2,1)S(1)}, bf16[384,384]{1,0:T(8,128)(2,1)S(1)}, bf16[3,384,768]{2,1,0:T(8,128)(2,1)S(1)}, f32[384,384]{1,0:T(8,128)S(1)}, bf16[768,768]{1,0:T(8,128)(2,1)S(1)}) custom-call(bf16[3,768,384]{2,1,0:T(8,128)(2,1)S(1)} %get-tuple-element.19.refs_0_.refs_1_, bf16[768,384]{1,0:T(8,128)(2,1)S(1)} %get-tuple-element.22.refs_1_, ...), custom_call_target="tpu_custom_call" | custom-call | flops 9059696640 | bytes 3538944 | tf_op jit(solution)/shard_map/second/pallas_call | solution.py:266
  8.3 2.0 %collective-permute-done.1.refs_8_ = bf16[384,384]{1,0:T(8,128)(2,1)S(1)} collective-permute-done((bf16[384,384]{1,0:T(8,128)(2,1)S(1)}, bf16[384,384]{1,0:T(8,128)(2,1)S(1)}, u32[]{:S(2)}, u32[]{:S(2)}) %collective-permute-start.1) | collective-permute-done | bytes 294944 | tf_op jit(solution)/shard_map/ppermute | solution.py:264
  10.3 1.3 %collective-permute-start.2 = (bf16[384,384]{1,0:T(8,128)(2,1)S(1)}, bf16[384,384]{1,0:T(8,128)(2,1)S(1)}, u32[]{:S(2)}, u32[]{:S(2)}) collective-permute-start(bf16[384,384]{1,0:T(8,128)(2,1)S(1)} %collective-permute-done.1.refs_8_), channel_id=1, source_target_pairs={{64,480},{160,256},{320,224},{416,0},{65,481},{161,257},{321,225},... | collective-permute-start | bytes 884744 | tf_op jit(solution)/shard_map/ppermute | solution.py:283
  11.6 15.2 %collective-permute-start.3 = (bf16[384,384]{1,0:T(8,128)(2,1)S(1)}, bf16[384,384]{1,0:T(8,128)(2,1)S(1)}, u32[]{:S(2)}, u32[]{:S(2)}) collective-permute-start(bf16[384,384]{1,0:T(8,128)(2,1)S(1)} %get-tuple-element.32), channel_id=1, source_target_pairs={{0,480},{224,256},{256,224},{480,0},{1,481},{225,257},{257,225},{4... | collective-permute-start | bytes 884744 | tf_op jit(solution)/shard_map/ppermute | solution.py:284
  26.8 0.0 collective-permute-done.refs_7_
  26.9 0.1 near.1
  26.9 1.3 %collective-permute-start.4 = (bf16[768,384]{1,0:T(8,128)(2,1)S(1)}, bf16[768,384]{1,0:T(8,128)(2,1)S(1)}, u32[]{:S(2)}, u32[]{:S(2)}) collective-permute-start(bf16[768,384]{1,0:T(8,128)(2,1)S(1)} %get-tuple-element.34), channel_id=1, source_target_pairs={{0,32},{32,64},{64,96},{96,128},{128,160},{160,192},{192,224},{256... | collective-permute-start | bytes 1769480 | tf_op jit(solution)/shard_map/ppermute | solution.py:296
  28.2 12.7 %collective-permute-done.2.refs_8_.refs_2_ = bf16[384,384]{1,0:T(8,128)(2,1)S(1)} collective-permute-done((bf16[384,384]{1,0:T(8,128)(2,1)S(1)}, bf16[384,384]{1,0:T(8,128)(2,1)S(1)}, u32[]{:S(2)}, u32[]{:S(2)}) %collective-permute-start.2) | collective-permute-done | bytes 294944 | tf_op jit(solution)/shard_map/ppermute | solution.py:283
  40.9 0.0 collective-permute-done.3.refs_9_.refs_3_
  41.0 3.8 %far.1 = (bf16[3,768,384]{2,1,0:T(8,128)(2,1)}, f32[8,128]{1,0:T(8,128)S(1)}) custom-call(bf16[3,768,384]{2,1,0:T(8,128)(2,1)} %get-tuple-element.29.refs_0_, bf16[3,768,384]{2,1,0:T(8,128)(2,1)S(1)} %get-tuple-element.19.refs_0_.refs_1_, bf16[3,384,512]{2,1,0:T(8,128)(2,1)S(1)} %get-tuple-element.20.refs_1_.refs_2_, ...), custom_call_target="tpu_custom_call", output_to_operand_aliasing={{0}: (0, {})} | custom-call | flops 9059696640 | bytes 3538944 | tf_op jit(solution)/shard_map/far/pallas_call | solution.py:297
  44.8 0.0 collective-permute-done.4.refs_1_
  44.8 0.8 %emit.1 = bf16[768,384]{1,0:T(8,128)(2,1)} custom-call(f32[8,128]{1,0:T(8,128)S(1)} %get-tuple-element.33.refs_0_, bf16[768,384]{1,0:T(8,128)(2,1)S(1)} %collective-permute-done.4.refs_1_, bf16[384,384]{1,0:T(8,128)(2,1)S(1)} %collective-permute-done.2.refs_8_.refs_2_, bf16[384,384]{1,0:T(8,128)(2,1)S(1)} %collective-permute-done.3.refs_9_.refs_3_), custom_call_target="tpu_custom_call" | custom-call | flops 1 | bytes 3538944 | tf_op jit(solution)/shard_map/emit/pallas_call | solution.py:308
Async XLA Ops:
  0.6 2.3 %copy-start = (bf16[1,768,384]{2,1,0:T(8,128)(2,1)S(1)}, bf16[1,768,384]{2,1,0:T(8,128)(2,1)}, u32[]{:S(2)}) copy-start(bf16[1,768,384]{2,1,0:T(8,128)(2,1)} %param.3) | copy-start | bytes 1769476
  3.1 7.2 %collective-permute-start.1 = (bf16[384,384]{1,0:T(8,128)(2,1)S(1)}, bf16[384,384]{1,0:T(8,128)(2,1)S(1)}, u32[]{:S(2)}, u32[]{:S(2)}) collective-permute-start(bf16[384,384]{1,0:T(8,128)(2,1)S(1)} %get-tuple-element.28), channel_id=1, source_target_pairs={{0,64},{224,160},{256,320},{480,416},{1,65},{225,161},{257,321},{4... | collective-permute-start | bytes 884744 | tf_op jit(solution)/shard_map/ppermute | solution.py:264
  5.5 21.4 %collective-permute-start = (bf16[768,384]{1,0:T(8,128)(2,1)S(1)}, bf16[768,384]{1,0:T(8,128)(2,1)S(1)}, u32[]{:S(2)}, u32[]{:S(2)}) collective-permute-start(bf16[768,384]{1,0:T(8,128)(2,1)S(1)} %get-tuple-element.22.refs_1_), channel_id=1, source_target_pairs={{32,0},{64,32},{96,64},{128,96},{160,128},{192,160},{224,192},{288... | collective-permute-start | bytes 1769480 | tf_op jit(solution)/shard_map/ppermute | solution.py:265
  10.3 30.6 %collective-permute-start.2 = (bf16[384,384]{1,0:T(8,128)(2,1)S(1)}, bf16[384,384]{1,0:T(8,128)(2,1)S(1)}, u32[]{:S(2)}, u32[]{:S(2)}) collective-permute-start(bf16[384,384]{1,0:T(8,128)(2,1)S(1)} %collective-permute-done.1.refs_8_), channel_id=1, source_target_pairs={{64,480},{160,256},{320,224},{416,0},{65,481},{161,257},{321,225},... | collective-permute-start | bytes 884744 | tf_op jit(solution)/shard_map/ppermute | solution.py:283
  11.6 29.4 %collective-permute-start.3 = (bf16[384,384]{1,0:T(8,128)(2,1)S(1)}, bf16[384,384]{1,0:T(8,128)(2,1)S(1)}, u32[]{:S(2)}, u32[]{:S(2)}) collective-permute-start(bf16[384,384]{1,0:T(8,128)(2,1)S(1)} %get-tuple-element.32), channel_id=1, source_target_pairs={{0,480},{224,256},{256,224},{480,0},{1,481},{225,257},{257,225},{4... | collective-permute-start | bytes 884744 | tf_op jit(solution)/shard_map/ppermute | solution.py:284
  26.9 17.8 %collective-permute-start.4 = (bf16[768,384]{1,0:T(8,128)(2,1)S(1)}, bf16[768,384]{1,0:T(8,128)(2,1)S(1)}, u32[]{:S(2)}, u32[]{:S(2)}) collective-permute-start(bf16[768,384]{1,0:T(8,128)(2,1)S(1)} %get-tuple-element.34), channel_id=1, source_target_pairs={{0,32},{32,64},{64,96},{96,128},{128,160},{160,192},{192,224},{256... | collective-permute-start | bytes 1769480 | tf_op jit(solution)/shard_map/ppermute | solution.py:296

commit v5 on v4

--- a/solution.py
+++ b/solution.py
@@ -176,21 +176,16 @@
         gradients(held, parts, grads_ref, *work)
 
 
-def far_kernel(half, _, *refs):
-    held, (first_ref, second_ref, relay_ref, direct_ref, grads_ref, token_ref), work = refs[:5], refs[5:11], refs[11:]
-    token_ref[...] = jnp.zeros_like(token_ref)
-    cut, length = first_ref.shape[0], held[4].shape[0]
-
-    @pl.when(lax.rem(lax.axis_index(SECTION), half) == half - 1)
-    def _():
-        parts = [(0, cut, first_ref, relay_ref), (cut, length, second_ref, direct_ref)]
-        gradients(held, parts, grads_ref, *work)
-
-
-def emit_kernel(half, _, near_ref, relay_ref, direct_ref, attn_ref, sem):
-    cut, length = relay_ref.shape[0], attn_ref.shape[0]
+def token_kernel(*refs):
+    refs[-1][...] = jnp.zeros_like(refs[-1])
+
+
+def far_kernel(half, _, __, *refs):
+    held, (first_ref, second_ref, relay_ref, direct_ref, near_ref, grads_ref, attn_ref), work = refs[:5], refs[5:12], refs[12:]
+    work, sem = work[:-1], work[-1]
+    cut, length = first_ref.shape[0], attn_ref.shape[0]
     place = lax.rem(lax.axis_index(SECTION), half)
-    parts = [(0, cut, relay_ref), (cut, length, direct_ref)]
+    parts = [(0, cut, first_ref, relay_ref), (cut, length, second_ref, direct_ref)]
 
     def send(k, source):
         return pltpu.make_async_copy(source, attn_ref.at[parts[k][0] : parts[k][1]], sem.at[k])
@@ -198,12 +193,16 @@
     @pl.when(place == 0)
     def _():
         for k, part in enumerate(parts):
-            send(k, part[2]).start()
+            send(k, part[3]).start()
 
     @pl.when(place != 0)
     def _():
         for k, part in enumerate(parts):
             send(k, near_ref.at[part[0] : part[1]]).start()
+
+    @pl.when(place == half - 1)
+    def _():
+        gradients(held, parts, grads_ref, *work)
 
     for k, part in enumerate(parts):
         send(k, near_ref.at[part[0] : part[1]]).wait()
@@ -294,27 +293,26 @@
         cost_estimate=cost(4 * work),
     )(*kept, near_dout, relay_hop)
     near_out = lax.ppermute(passed, SECTION, near_pairs(count, half, 1))
-    grads, token = pl.pallas_call(
+    token = pl.pallas_call(
+        token_kernel,
+        out_shape=jax.ShapeDtypeStruct((8, HD), jnp.float32),
+        in_specs=[ANY] * 2,
+        out_specs=VMEM,
+        name="token",
+        compiler_params=pltpu.CompilerParams(vmem_limit_bytes=2**20),
+        cost_estimate=cost(40 * work),
+    )(relay, direct)
+    grads, attn_out = pl.pallas_call(
         lambda *refs: far_kernel(half, *refs),
-        out_shape=(three, jax.ShapeDtypeStruct((8, HD), jnp.float32)),
-        in_specs=[HBM] + [VMEM] * 9,
-        out_specs=(HBM, VMEM),
-        scratch_shapes=scratch,
+        out_shape=(three, whole),
+        in_specs=[HBM, ANY] + [VMEM] * 10,
+        out_specs=(HBM, HBM),
+        scratch_shapes=[*scratch, pltpu.SemaphoreType.DMA((2,))],
         input_output_aliases={0: 0},
         name="far",
         compiler_params=params,
         cost_estimate=cost(40 * work),
-    )(grads, *kept, relay, direct)
-    attn_out = pl.pallas_call(
-        lambda *refs: emit_kernel(half, *refs),
-        out_shape=whole,
-        in_specs=[ANY] * 4,
-        out_specs=HBM,
-        scratch_shapes=[pltpu.SemaphoreType.DMA((2,))],
-        name="emit",
-        compiler_params=pltpu.CompilerParams(vmem_limit_bytes=2**20),
-        cost_estimate=cost(1),
-    )(token, near_out, relay, direct)
+    )(grads, token, *kept, relay, direct, near_out)
     return (attn_out[None], grads.transpose(1, 0, 2)[None])
 
 

time: 45.8 us -> 45 us (0.983)
  the two profiles are of different devices: /device:TPU:61 before, /device:TPU:63 now
where the time goes in v5:
time: 45 us; the launch traced here: 44.8 us
  starting transfers between devices  21.5 us (48%)
  waiting for transfers between devices  14.7 us (33%)
  Pallas kernels  7.83 us (17%)
  between operations  0.73 us (2%)
    ppermute x1, starting transfers between devices, on_device(): lax.ppermute(direct, SECTION, far_pairs(count, half, [(0, last), (last, 0...  15.2 us
    ppermute x1, waiting for transfers between devices, on_device(): lax.ppermute(relay, SECTION, far_pairs(count, half, [(2, last), (last - 2...  12.6 us
    pallas_call x1, Pallas kernels, on_device(): pl.pallas_call(lambda *refs: far_kernel(half, *refs), out_shape=(three, w...  3.83 us
    ppermute x1, starting transfers between devices, on_device(): lax.ppermute(relay, SECTION, same_pairs(count, half, [(0, 2), (last, last...  2.39 us
    pallas_call x1, Pallas kernels, on_device(): pl.pallas_call(first_kernel, out_shape=(part, jax.ShapeDtypeStruct((heads...  2.32 us
    ppermute x1, waiting for transfers between devices, on_device(): lax.ppermute(relay, SECTION, same_pairs(count, half, [(0, 2), (last, last...  2.01 us
    pallas_call x1, Pallas kernels, on_device(): pl.pallas_call(lambda *refs: second_kernel(half, *refs), out_shape=(whole...  1.5 us
    ppermute x1, starting transfers between devices, on_device(): near_dout = lax.ppermute(held_dout, SECTION, near_pairs(count, half, -1))  1.33 us
  transfers between devices with their start and end apart: 5, of which 3 were waited for; matrix products, arithmetic and copies ran while one was open for 0% of the time, Pallas kernels for 4%

profile of v5, /device:TPU:63, one launch (start us, length us, event | category | flops | bytes accessed | tf_op | source)
XLA Modules:
  0.0 44.8 jit_solution(17594210033450827341)
XLA Ops:
  0.6 0.0 copy-start
  0.6 2.3 %first.1 = (bf16[384,384]{1,0:T(8,128)(2,1)S(1)}, bf16[3,384,512]{2,1,0:T(8,128)(2,1)S(1)}, f32[384,384]{1,0:T(8,128)S(1)}, bf16[3,768,384]{2,1,0:T(8,128)(2,1)S(1)}) custom-call(bf16[3,768,384]{2,1,0:T(8,128)(2,1)} %bitcast.9), custom_call_target="tpu_custom_call" | custom-call | flops 226492416 | bytes 3538944 | tf_op jit(solution)/shard_map/first/pallas_call | solution.py:244
  3.0 0.0 copy-done
  3.0 0.1 pick.1
  3.1 2.4 %collective-permute-start.1 = (bf16[384,384]{1,0:T(8,128)(2,1)S(1)}, bf16[384,384]{1,0:T(8,128)(2,1)S(1)}, u32[]{:S(2)}, u32[]{:S(2)}) collective-permute-start(bf16[384,384]{1,0:T(8,128)(2,1)S(1)} %get-tuple-element.28), channel_id=1, source_target_pairs={{0,64},{224,160},{256,320},{480,416},{1,65},{225,161},{257,321},{4... | collective-permute-start | bytes 884744 | tf_op jit(solution)/shard_map/ppermute | solution.py:263
  5.5 1.3 %collective-permute-start = (bf16[768,384]{1,0:T(8,128)(2,1)S(1)}, bf16[768,384]{1,0:T(8,128)(2,1)S(1)}, u32[]{:S(2)}, u32[]{:S(2)}) collective-permute-start(bf16[768,384]{1,0:T(8,128)(2,1)S(1)} %get-tuple-element.22.refs_1_), channel_id=1, source_target_pairs={{32,0},{64,32},{96,64},{128,96},{160,128},{192,160},{224,192},{288... | collective-permute-start | bytes 1769480 | tf_op jit(solution)/shard_map/ppermute | solution.py:264
  6.8 1.5 %second.1 = (bf16[768,384]{1,0:T(8,128)(2,1)S(1)}, bf16[384,384]{1,0:T(8,128)(2,1)S(1)}, bf16[3,384,768]{2,1,0:T(8,128)(2,1)S(1)}, f32[384,384]{1,0:T(8,128)S(1)}, bf16[768,768]{1,0:T(8,128)(2,1)S(1)}) custom-call(bf16[3,768,384]{2,1,0:T(8,128)(2,1)S(1)} %get-tuple-element.19.refs_0_.refs_2_, bf16[768,384]{1,0:T(8,128)(2,1)S(1)} %get-tuple-element.22.refs_1_, ...), custom_call_target="tpu_custom_call" | custom-call | flops 9059696640 | bytes 3538944 | tf_op jit(solution)/shard_map/second/pallas_call | solution.py:265
  8.3 2.0 %collective-permute-done.1.refs_8_ = bf16[384,384]{1,0:T(8,128)(2,1)S(1)} collective-permute-done((bf16[384,384]{1,0:T(8,128)(2,1)S(1)}, bf16[384,384]{1,0:T(8,128)(2,1)S(1)}, u32[]{:S(2)}, u32[]{:S(2)}) %collective-permute-start.1) | collective-permute-done | bytes 294944 | tf_op jit(solution)/shard_map/ppermute | solution.py:263
  10.3 1.3 %collective-permute-start.2 = (bf16[384,384]{1,0:T(8,128)(2,1)S(1)}, bf16[384,384]{1,0:T(8,128)(2,1)S(1)}, u32[]{:S(2)}, u32[]{:S(2)}) collective-permute-start(bf16[384,384]{1,0:T(8,128)(2,1)S(1)} %collective-permute-done.1.refs_8_), channel_id=1, source_target_pairs={{64,480},{160,256},{320,224},{416,0},{65,481},{161,257},{321,225},... | collective-permute-start | bytes 884744 | tf_op jit(solution)/shard_map/ppermute | solution.py:282
  11.6 15.2 %collective-permute-start.3 = (bf16[384,384]{1,0:T(8,128)(2,1)S(1)}, bf16[384,384]{1,0:T(8,128)(2,1)S(1)}, u32[]{:S(2)}, u32[]{:S(2)}) collective-permute-start(bf16[384,384]{1,0:T(8,128)(2,1)S(1)} %get-tuple-element.32), channel_id=1, source_target_pairs={{0,480},{224,256},{256,224},{480,0},{1,481},{225,257},{257,225},{4... | collective-permute-start | bytes 884744 | tf_op jit(solution)/shard_map/ppermute | solution.py:283
  26.8 0.0 collective-permute-done.refs_7_
  26.9 0.1 near.1
  26.9 1.3 %collective-permute-start.4 = (bf16[768,384]{1,0:T(8,128)(2,1)S(1)}, bf16[768,384]{1,0:T(8,128)(2,1)S(1)}, u32[]{:S(2)}, u32[]{:S(2)}) collective-permute-start(bf16[768,384]{1,0:T(8,128)(2,1)S(1)} %get-tuple-element.33), channel_id=1, source_target_pairs={{0,32},{32,64},{64,96},{96,128},{128,160},{160,192},{192,224},{256... | collective-permute-start | bytes 1769480 | tf_op jit(solution)/shard_map/ppermute | solution.py:295
  28.2 12.6 %collective-permute-done.2.refs_0_.refs_9_ = bf16[384,384]{1,0:T(8,128)(2,1)S(1)} collective-permute-done((bf16[384,384]{1,0:T(8,128)(2,1)S(1)}, bf16[384,384]{1,0:T(8,128)(2,1)S(1)}, u32[]{:S(2)}, u32[]{:S(2)}) %collective-permute-start.2) | collective-permute-done | bytes 294944 | tf_op jit(solution)/shard_map/ppermute | solution.py:282
  40.9 0.1 collective-permute-done.3.refs_1_.refs_10_
  41.0 0.0 collective-permute-done.4.refs_11_
  41.0 3.8 %far.1 = (bf16[3,768,384]{2,1,0:T(8,128)(2,1)}, bf16[768,384]{1,0:T(8,128)(2,1)}) custom-call(bf16[3,768,384]{2,1,0:T(8,128)(2,1)} %get-tuple-element.29.refs_0_, f32[8,128]{1,0:T(8,128)S(1)} %token_.1.refs_1_, bf16[3,768,384]{2,1,0:T(8,128)(2,1)S(1)} %get-tuple-element.19.refs_0_.refs_2_, ...), custom_call_target="tpu_custom_call", output_to_operand_aliasing={{0}: (0, {})} | custom-call | flops 9059696640 | bytes 3538944 | tf_op jit(solution)/shard_map/far/pallas_call | solution.py:305
  (1 shorter events, 0.0 us)
Async XLA Ops:
  0.6 2.3 %copy-start = (bf16[1,768,384]{2,1,0:T(8,128)(2,1)S(1)}, bf16[1,768,384]{2,1,0:T(8,128)(2,1)}, u32[]{:S(2)}) copy-start(bf16[1,768,384]{2,1,0:T(8,128)(2,1)} %param.3) | copy-start | bytes 1769476
  3.1 7.2 %collective-permute-start.1 = (bf16[384,384]{1,0:T(8,128)(2,1)S(1)}, bf16[384,384]{1,0:T(8,128)(2,1)S(1)}, u32[]{:S(2)}, u32[]{:S(2)}) collective-permute-start(bf16[384,384]{1,0:T(8,128)(2,1)S(1)} %get-tuple-element.28), channel_id=1, source_target_pairs={{0,64},{224,160},{256,320},{480,416},{1,65},{225,161},{257,321},{4... | collective-permute-start | bytes 884744 | tf_op jit(solution)/shard_map/ppermute | solution.py:263
  5.5 21.4 %collective-permute-start = (bf16[768,384]{1,0:T(8,128)(2,1)S(1)}, bf16[768,384]{1,0:T(8,128)(2,1)S(1)}, u32[]{:S(2)}, u32[]{:S(2)}) collective-permute-start(bf16[768,384]{1,0:T(8,128)(2,1)S(1)} %get-tuple-element.22.refs_1_), channel_id=1, source_target_pairs={{32,0},{64,32},{96,64},{128,96},{160,128},{192,160},{224,192},{288... | collective-permute-start | bytes 1769480 | tf_op jit(solution)/shard_map/ppermute | solution.py:264
  10.3 30.6 %collective-permute-start.2 = (bf16[384,384]{1,0:T(8,128)(2,1)S(1)}, bf16[384,384]{1,0:T(8,128)(2,1)S(1)}, u32[]{:S(2)}, u32[]{:S(2)}) collective-permute-start(bf16[384,384]{1,0:T(8,128)(2,1)S(1)} %collective-permute-done.1.refs_8_), channel_id=1, source_target_pairs={{64,480},{160,256},{320,224},{416,0},{65,481},{161,257},{321,225},... | collective-permute-start | bytes 884744 | tf_op jit(solution)/shard_map/ppermute | solution.py:282
  11.6 29.4 %collective-permute-start.3 = (bf16[384,384]{1,0:T(8,128)(2,1)S(1)}, bf16[384,384]{1,0:T(8,128)(2,1)S(1)}, u32[]{:S(2)}, u32[]{:S(2)}) collective-permute-start(bf16[384,384]{1,0:T(8,128)(2,1)S(1)} %get-tuple-element.32), channel_id=1, source_target_pairs={{0,480},{224,256},{256,224},{480,0},{1,481},{225,257},{257,225},{4... | collective-permute-start | bytes 884744 | tf_op jit(solution)/shard_map/ppermute | solution.py:283
  26.9 14.0 %collective-permute-start.4 = (bf16[768,384]{1,0:T(8,128)(2,1)S(1)}, bf16[768,384]{1,0:T(8,128)(2,1)S(1)}, u32[]{:S(2)}, u32[]{:S(2)}) collective-permute-start(bf16[768,384]{1,0:T(8,128)(2,1)S(1)} %get-tuple-element.33), channel_id=1, source_target_pairs={{0,32},{32,64},{64,96},{96,128},{128,160},{160,192},{192,224},{256... | collective-permute-start | bytes 1769480 | tf_op jit(solution)/shard_map/ppermute | solution.py:295

commit v6 on v5

--- a/solution.py
+++ b/solution.py
@@ -130,6 +130,13 @@
         if stop > cut:
             pieces.append(late_ref[head, max(start, cut) - cut : stop - cut, cols])
         return pieces[0] if len(pieces) == 1 else jnp.concatenate(pieces, axis=0)
+
+    def leave(which, head, at):
+        copy = pltpu.make_async_copy(
+            stage_ref.at[which, :, at], grads_ref.at[which, :, at], grads_sem.at[3 * head + which]
+        )
+        copy.start()
+        return copy
 
     for head in range(heads):
         at, wide = lanes(head), lanes(head, 2)
@@ -149,6 +156,7 @@
             dq = dot_nn(grad_s, qkv_ref[1, k_at, at])
             sums_ref[0, q_at] = dq if first == 0 else sums_ref[0, q_at] + dq
         stage_ref[0, :, at] = (sums_ref[0] * SCALE).astype(jnp.bfloat16)
+        copies.append(leave(0, head, at))
         for first in reversed(range(0, length, BLK)):
             q_at, k_at = slice(first, first + BLK), slice(0, first + BLK)
             dk = dot_tn(scores_ref[q_at, k_at], qkv_ref[0, q_at, at])
@@ -157,10 +165,10 @@
             sums_ref[1, k_at] = dk if last else sums_ref[1, k_at] + dk
             sums_ref[2, k_at] = dv if last else sums_ref[2, k_at] + dv
         stage_ref[1, :, at] = (sums_ref[1] * SCALE).astype(jnp.bfloat16)
+        copies.append(leave(1, head, at))
         stage_ref[2, :, at] = sums_ref[2].astype(jnp.bfloat16)
-        copy = pltpu.make_async_copy(stage_ref.at[:, :, at], grads_ref.at[:, :, at], grads_sem.at[head])
-        copy.start()
-        copies.append(copy)
+        copies.append(leave(2, head, at))
+
     for copy in copies:
         copy.wait()
 
@@ -235,7 +243,7 @@
         pltpu.VMEM(qkv.shape, bf16),
         pltpu.VMEM((length, length), bf16),
         pltpu.VMEM((3, length, HD), jnp.float32),
-        pltpu.SemaphoreType.DMA((heads,)),
+        pltpu.SemaphoreType.DMA((3 * heads,)),
     ]
 
     def cost(flops):

time: 45 us -> 45 us (level)
  no operation moved by 1% of the time
where the time goes in v6:
time: 45 us; the launch traced here: 44.8 us
  starting transfers between devices  21.5 us (48%)
  waiting for transfers between devices  14.7 us (33%)
  Pallas kernels  7.84 us (17%)
  between operations  0.73 us (2%)
    ppermute x1, starting transfers between devices, on_device(): lax.ppermute(direct, SECTION, far_pairs(count, half, [(0, last), (last, 0...  15.2 us
    ppermute x1, waiting for transfers between devices, on_device(): lax.ppermute(relay, SECTION, far_pairs(count, half, [(2, last), (last - 2...  12.6 us
    pallas_call x1, Pallas kernels, on_device(): pl.pallas_call(lambda *refs: far_kernel(half, *refs), out_shape=(three, w...  3.79 us
    ppermute x1, starting transfers between devices, on_device(): lax.ppermute(relay, SECTION, same_pairs(count, half, [(0, 2), (last, last...  2.39 us
    pallas_call x1, Pallas kernels, on_device(): pl.pallas_call(first_kernel, out_shape=(part, jax.ShapeDtypeStruct((heads...  2.32 us
    ppermute x1, waiting for transfers between devices, on_device(): lax.ppermute(relay, SECTION, same_pairs(count, half, [(0, 2), (last, last...  2.01 us
    pallas_call x1, Pallas kernels, on_device(): pl.pallas_call(lambda *refs: second_kernel(half, *refs), out_shape=(whole...  1.5 us
    ppermute x1, starting transfers between devices, on_device(): near_dout = lax.ppermute(held_dout, SECTION, near_pairs(count, half, -1))  1.33 us
  transfers between devices with their start and end apart: 5, of which 3 were waited for; matrix products, arithmetic and copies ran while one was open for 0% of the time, Pallas kernels for 4%

profile of v6, /device:TPU:63, one launch (start us, length us, event | category | flops | bytes accessed | tf_op | source)
XLA Modules:
  0.0 44.8 jit_solution(17914576320178119213)
XLA Ops:
  0.6 0.0 copy-start
  0.6 2.3 %first.1 = (bf16[384,384]{1,0:T(8,128)(2,1)S(1)}, bf16[3,384,512]{2,1,0:T(8,128)(2,1)S(1)}, f32[384,384]{1,0:T(8,128)S(1)}, bf16[3,768,384]{2,1,0:T(8,128)(2,1)S(1)}) custom-call(bf16[3,768,384]{2,1,0:T(8,128)(2,1)} %bitcast.9), custom_call_target="tpu_custom_call" | custom-call | flops 226492416 | bytes 3538944 | tf_op jit(solution)/shard_map/first/pallas_call | solution.py:252
  3.0 0.0 copy-done
  3.0 0.1 pick.1
  3.1 2.4 %collective-permute-start.1 = (bf16[384,384]{1,0:T(8,128)(2,1)S(1)}, bf16[384,384]{1,0:T(8,128)(2,1)S(1)}, u32[]{:S(2)}, u32[]{:S(2)}) collective-permute-start(bf16[384,384]{1,0:T(8,128)(2,1)S(1)} %get-tuple-element.28), channel_id=1, source_target_pairs={{0,64},{224,160},{256,320},{480,416},{1,65},{225,161},{257,321},{4... | collective-permute-start | bytes 884744 | tf_op jit(solution)/shard_map/ppermute | solution.py:271
  5.5 1.3 %collective-permute-start = (bf16[768,384]{1,0:T(8,128)(2,1)S(1)}, bf16[768,384]{1,0:T(8,128)(2,1)S(1)}, u32[]{:S(2)}, u32[]{:S(2)}) collective-permute-start(bf16[768,384]{1,0:T(8,128)(2,1)S(1)} %get-tuple-element.22.refs_1_), channel_id=1, source_target_pairs={{32,0},{64,32},{96,64},{128,96},{160,128},{192,160},{224,192},{288... | collective-permute-start | bytes 1769480 | tf_op jit(solution)/shard_map/ppermute | solution.py:272
  6.8 1.5 %second.1 = (bf16[768,384]{1,0:T(8,128)(2,1)S(1)}, bf16[384,384]{1,0:T(8,128)(2,1)S(1)}, bf16[3,384,768]{2,1,0:T(8,128)(2,1)S(1)}, f32[384,384]{1,0:T(8,128)S(1)}, bf16[768,768]{1,0:T(8,128)(2,1)S(1)}) custom-call(bf16[3,768,384]{2,1,0:T(8,128)(2,1)S(1)} %get-tuple-element.19.refs_0_.refs_2_, bf16[768,384]{1,0:T(8,128)(2,1)S(1)} %get-tuple-element.22.refs_1_, ...), custom_call_target="tpu_custom_call" | custom-call | flops 9059696640 | bytes 3538944 | tf_op jit(solution)/shard_map/second/pallas_call | solution.py:273
  8.3 2.0 %collective-permute-done.1.refs_8_ = bf16[384,384]{1,0:T(8,128)(2,1)S(1)} collective-permute-done((bf16[384,384]{1,0:T(8,128)(2,1)S(1)}, bf16[384,384]{1,0:T(8,128)(2,1)S(1)}, u32[]{:S(2)}, u32[]{:S(2)}) %collective-permute-start.1) | collective-permute-done | bytes 294944 | tf_op jit(solution)/shard_map/ppermute | solution.py:271
  10.3 1.3 %collective-permute-start.2 = (bf16[384,384]{1,0:T(8,128)(2,1)S(1)}, bf16[384,384]{1,0:T(8,128)(2,1)S(1)}, u32[]{:S(2)}, u32[]{:S(2)}) collective-permute-start(bf16[384,384]{1,0:T(8,128)(2,1)S(1)} %collective-permute-done.1.refs_8_), channel_id=1, source_target_pairs={{64,480},{160,256},{320,224},{416,0},{65,481},{161,257},{321,225},... | collective-permute-start | bytes 884744 | tf_op jit(solution)/shard_map/ppermute | solution.py:290
  11.6 15.2 %collective-permute-start.3 = (bf16[384,384]{1,0:T(8,128)(2,1)S(1)}, bf16[384,384]{1,0:T(8,128)(2,1)S(1)}, u32[]{:S(2)}, u32[]{:S(2)}) collective-permute-start(bf16[384,384]{1,0:T(8,128)(2,1)S(1)} %get-tuple-element.32), channel_id=1, source_target_pairs={{0,480},{224,256},{256,224},{480,0},{1,481},{225,257},{257,225},{4... | collective-permute-start | bytes 884744 | tf_op jit(solution)/shard_map/ppermute | solution.py:291
  26.8 0.0 collective-permute-done.refs_7_
  26.9 0.1 near.1
  27.0 1.3 %collective-permute-start.4 = (bf16[768,384]{1,0:T(8,128)(2,1)S(1)}, bf16[768,384]{1,0:T(8,128)(2,1)S(1)}, u32[]{:S(2)}, u32[]{:S(2)}) collective-permute-start(bf16[768,384]{1,0:T(8,128)(2,1)S(1)} %get-tuple-element.33), channel_id=1, source_target_pairs={{0,32},{32,64},{64,96},{96,128},{128,160},{160,192},{192,224},{256... | collective-permute-start | bytes 1769480 | tf_op jit(solution)/shard_map/ppermute | solution.py:303
  28.3 12.6 %collective-permute-done.2.refs_0_.refs_9_ = bf16[384,384]{1,0:T(8,128)(2,1)S(1)} collective-permute-done((bf16[384,384]{1,0:T(8,128)(2,1)S(1)}, bf16[384,384]{1,0:T(8,128)(2,1)S(1)}, u32[]{:S(2)}, u32[]{:S(2)}) %collective-permute-start.2) | collective-permute-done | bytes 294944 | tf_op jit(solution)/shard_map/ppermute | solution.py:290
  40.9 0.1 collective-permute-done.3.refs_1_.refs_10_
  41.0 0.0 collective-permute-done.4.refs_11_
  41.0 3.8 %far.1 = (bf16[3,768,384]{2,1,0:T(8,128)(2,1)}, bf16[768,384]{1,0:T(8,128)(2,1)}) custom-call(bf16[3,768,384]{2,1,0:T(8,128)(2,1)} %get-tuple-element.29.refs_0_, f32[8,128]{1,0:T(8,128)S(1)} %token_.1.refs_1_, bf16[3,768,384]{2,1,0:T(8,128)(2,1)S(1)} %get-tuple-element.19.refs_0_.refs_2_, ...), custom_call_target="tpu_custom_call", output_to_operand_aliasing={{0}: (0, {})} | custom-call | flops 9059696640 | bytes 3538944 | tf_op jit(solution)/shard_map/far/pallas_call | solution.py:313
  (1 shorter events, 0.0 us)
Async XLA Ops:
  0.6 2.3 %copy-start = (bf16[1,768,384]{2,1,0:T(8,128)(2,1)S(1)}, bf16[1,768,384]{2,1,0:T(8,128)(2,1)}, u32[]{:S(2)}) copy-start(bf16[1,768,384]{2,1,0:T(8,128)(2,1)} %param.3) | copy-start | bytes 1769476
  3.1 7.2 %collective-permute-start.1 = (bf16[384,384]{1,0:T(8,128)(2,1)S(1)}, bf16[384,384]{1,0:T(8,128)(2,1)S(1)}, u32[]{:S(2)}, u32[]{:S(2)}) collective-permute-start(bf16[384,384]{1,0:T(8,128)(2,1)S(1)} %get-tuple-element.28), channel_id=1, source_target_pairs={{0,64},{224,160},{256,320},{480,416},{1,65},{225,161},{257,321},{4... | collective-permute-start | bytes 884744 | tf_op jit(solution)/shard_map/ppermute | solution.py:271
  5.5 21.4 %collective-permute-start = (bf16[768,384]{1,0:T(8,128)(2,1)S(1)}, bf16[768,384]{1,0:T(8,128)(2,1)S(1)}, u32[]{:S(2)}, u32[]{:S(2)}) collective-permute-start(bf16[768,384]{1,0:T(8,128)(2,1)S(1)} %get-tuple-element.22.refs_1_), channel_id=1, source_target_pairs={{32,0},{64,32},{96,64},{128,96},{160,128},{192,160},{224,192},{288... | collective-permute-start | bytes 1769480 | tf_op jit(solution)/shard_map/ppermute | solution.py:272
  10.3 30.6 %collective-permute-start.2 = (bf16[384,384]{1,0:T(8,128)(2,1)S(1)}, bf16[384,384]{1,0:T(8,128)(2,1)S(1)}, u32[]{:S(2)}, u32[]{:S(2)}) collective-permute-start(bf16[384,384]{1,0:T(8,128)(2,1)S(1)} %collective-permute-done.1.refs_8_), channel_id=1, source_target_pairs={{64,480},{160,256},{320,224},{416,0},{65,481},{161,257},{321,225},... | collective-permute-start | bytes 884744 | tf_op jit(solution)/shard_map/ppermute | solution.py:290
  11.6 29.4 %collective-permute-start.3 = (bf16[384,384]{1,0:T(8,128)(2,1)S(1)}, bf16[384,384]{1,0:T(8,128)(2,1)S(1)}, u32[]{:S(2)}, u32[]{:S(2)}) collective-permute-start(bf16[384,384]{1,0:T(8,128)(2,1)S(1)} %get-tuple-element.32), channel_id=1, source_target_pairs={{0,480},{224,256},{256,224},{480,0},{1,481},{225,257},{257,225},{4... | collective-permute-start | bytes 884744 | tf_op jit(solution)/shard_map/ppermute | solution.py:291
  27.0 14.0 %collective-permute-start.4 = (bf16[768,384]{1,0:T(8,128)(2,1)S(1)}, bf16[768,384]{1,0:T(8,128)(2,1)S(1)}, u32[]{:S(2)}, u32[]{:S(2)}) collective-permute-start(bf16[768,384]{1,0:T(8,128)(2,1)S(1)} %get-tuple-element.33), channel_id=1, source_target_pairs={{0,32},{32,64},{64,96},{96,128},{128,160},{160,192},{192,224},{256... | collective-permute-start | bytes 1769480 | tf_op jit(solution)/shard_map/ppermute | solution.py:303
